TPU v7x, 32 devices: a whole 2x2x4 slice. The times are simulated.
32 devices in a mesh: expert: 16 (over z, y, x), tensor: 2 (over core).
Axes of the slice: x: 2, y: 2, z: 4, core: 2. Of those that a mesh axis runs over, the one named last changes fastest.
Arguments:
- cotangent: bfloat16 [2048, 4096], P('expert', 'tensor'), may hold values from -1.5 to 1.5
- routes: int32 [2048, 2], P('expert'), may hold values from 0 to 15, all different within a row; in each aligned block of 128 rows (0 to 127, 128 to 255, ...) at most 32 rows name the same one
- router_weight: float32 [2048, 2], P('expert'), may hold values from 0.1 to 0.9
- clients: int32 [2048], P('expert'), may hold values from 0 to 3
- gate_preactivation: bfloat16 [16, 512, 3072], P('expert', None, 'tensor'), may hold values from -6 to 6
- up_preactivation: bfloat16 [16, 512, 3072], P('expert', None, 'tensor'), may hold values from -6 to 6
- down_matrix: bfloat16 [16, 3072, 4096], P('expert', 'tensor'), may hold values from -0.109375 to 0.109375
- adapter_input_maps: bfloat16 [16, 3072, 64], P('expert', 'tensor'), may hold values from -0.359375 to 0.359375
- adapter_output_maps: bfloat16 [16, 64, 4096], P('expert', None, 'tensor'), may hold values from -0.09375 to 0.09375
Outputs:
- gate_grad: float32 [2048, 2], P('expert')
- grad_gate_pre: bfloat16 [16, 512, 3072], P('expert', None, 'tensor')
- grad_up_pre: bfloat16 [16, 512, 3072], P('expert', None, 'tensor')
- grad_lora_a: float32 [16, 3072, 64], P('expert', 'tensor')
- grad_lora_b: float32 [16, 64, 4096], P('expert', None, 'tensor')
Inputs may be any that keep to these rules, and one draw needn't show every extreme that they name: `routes`: the 2 experts of a token differ. Among the 128 tokens of one device no expert is named more than 32 times, and in every draw some expert is named exactly 32 times by the tokens of some device.
All inputs are finite; a program needn't handle non-finite values.
Results may differ from a plain program's by a relative error of at most 0.0049.
Values may be sent and summed in bfloat16 or wider, within the bound.
A program may use at most 64 MiB of HBM per device.

v0:
```python
import jax
import jax.numpy as jnp
from jax import lax
from jax.sharding import PartitionSpec as P

ADAPTER_RANK = 16


adapter_scale = 2.0


def silu_parts(gate):
    sig = jax.nn.sigmoid(gate)
    return (gate * sig, sig * (1.0 + gate * (1.0 - sig)))


def local(
    cotangent,
    routes,
    router_weight,
    clients,
    gate_preactivation,
    up_preactivation,
    down_matrix,
    adapter_input_maps,
    adapter_output_maps,
):
    experts = lax.axis_size("expert")
    tok_rows = cotangent.shape[0]
    width = cotangent.shape[1]
    picks_per = routes.shape[1]
    slots = gate_preactivation.shape[1]
    per_source = slots // experts
    adapter_groups = adapter_input_maps.shape[2] // ADAPTER_RANK
    picks = routes.reshape(-1)
    onehot = (picks[:, None] == jnp.arange(experts, dtype=jnp.int32)).astype(jnp.int32)
    before = jnp.cumsum(onehot, axis=0) - onehot
    rank = jnp.sum(before * onehot, axis=1)
    slot = picks * per_source + rank
    owner = jnp.arange(tok_rows * picks_per, dtype=jnp.int32) // picks_per
    weight_slots = (
        jnp.zeros((experts * per_source,), jnp.float32)
        .at[slot]
        .set(router_weight.reshape(-1))
        .reshape(experts, per_source)
    )
    client_hot = (clients[owner][:, None] == jnp.arange(adapter_groups, dtype=jnp.int32)).astype(
        jnp.float32
    )
    chosen_slots = (
        jnp.zeros((experts * per_source, adapter_groups), jnp.float32)
        .at[slot]
        .set(client_hot)
        .reshape(experts, per_source, adapter_groups)
    )
    weight_in, chosen_in = (
        lax.all_to_all(weight_slots, "expert", split_axis=0, concat_axis=0, tiled=True),
        lax.all_to_all(chosen_slots, "expert", split_axis=0, concat_axis=0, tiled=True),
    )
    whole = lax.all_gather(cotangent, "tensor", axis=1, tiled=True)
    full_width = whole.shape[1]
    buffer = jnp.zeros((experts * per_source, full_width), whole.dtype).at[slot].set(whole[owner])
    arrived = lax.all_to_all(
        buffer.reshape(experts, per_source, full_width),
        "expert",
        split_axis=0,
        concat_axis=0,
        tiled=True,
    )
    token_rows = arrived.reshape(slots, full_width)
    part = lax.dynamic_slice_in_dim(token_rows, lax.axis_index("tensor") * width, width, 1)
    pick_weight = weight_in.reshape(slots)
    client_mask = jnp.repeat(chosen_in.reshape(slots, adapter_groups), ADAPTER_RANK, axis=1)
    act, slope = silu_parts(gate_preactivation[0].astype(jnp.float32))
    up_full = up_preactivation[0].astype(jnp.float32)
    hidden_units = act * up_full
    hidden_lowrank = hidden_units.astype(jnp.bfloat16)
    contract_dims = (((1,), (1,)), ((), ()))
    row_dimensions = (((0,), (0,)), ((), ()))
    frozen_output = lax.dot_general(
        token_rows, down_matrix[0], contract_dims, preferred_element_type=jnp.float32
    )
    projected_piece = (
        jnp.dot(hidden_lowrank, adapter_input_maps[0], preferred_element_type=jnp.float32)
        * client_mask
    )
    local_terms = jnp.sum(hidden_units * frozen_output, axis=1)
    output_map_whole = lax.all_gather(adapter_output_maps[0], "tensor", axis=1, tiled=True)
    adapter_output = (
        lax.dot_general(
            token_rows, output_map_whole, contract_dims, preferred_element_type=jnp.float32
        )
        * client_mask
    )
    projected_rows, router_products = lax.psum((projected_piece, local_terms), "tensor")
    backward_result = lax.dot_general(
        adapter_output.astype(jnp.bfloat16),
        adapter_input_maps[0],
        contract_dims,
        preferred_element_type=jnp.float32,
    )
    hidden_gradient = pick_weight[:, None] * (frozen_output + adapter_scale * backward_result)
    gate_gradient = (hidden_gradient * up_full * slope).astype(jnp.bfloat16)
    up_gradient = (hidden_gradient * act).astype(jnp.bfloat16)
    input_map_gradient = adapter_scale * lax.dot_general(
        hidden_lowrank,
        (pick_weight[:, None] * adapter_output).astype(jnp.bfloat16),
        row_dimensions,
        preferred_element_type=jnp.float32,
    )
    output_map_gradient = adapter_scale * lax.dot_general(
        (pick_weight[:, None] * projected_rows).astype(jnp.bfloat16),
        part,
        row_dimensions,
        preferred_element_type=jnp.float32,
    )
    slot_gradient = router_products + adapter_scale * jnp.sum(
        projected_rows * adapter_output, axis=1
    )
    returned = lax.all_to_all(
        slot_gradient.reshape(experts, per_source),
        "expert",
        split_axis=0,
        concat_axis=0,
        tiled=True,
    )
    gate_grad = returned.reshape(-1)[slot].reshape(tok_rows, picks_per)
    return (
        gate_grad,
        gate_gradient[None],
        up_gradient[None],
        input_map_gradient[None],
        output_map_gradient[None],
    )


def solution(mesh):
    in_specs = (
        P("expert", "tensor"),
        P("expert", None),
        P("expert", None),
        P("expert"),
        P("expert", None, "tensor"),
        P("expert", None, "tensor"),
        P("expert", "tensor", None),
        P("expert", "tensor", None),
        P("expert", None, "tensor"),
    )
    out_specs = (
        P("expert", None),
        P("expert", None, "tensor"),
        P("expert", None, "tensor"),
        P("expert", "tensor", None),
        P("expert", None, "tensor"),
    )
    return jax.shard_map(local, mesh=mesh, in_specs=in_specs, out_specs=out_specs, check_vma=False)
```

profile of v0, /device:TPU:0, one launch (start us, length us, event | category | flops | bytes accessed | tf_op | source)
XLA Modules:
  0.0 191.4 jit_solution(16368690577501239698)
XLA Ops:
  7.2 0.7 all-gather.3.cloned.1.call-update
  7.9 0.8 copy.29
  9.0 0.7 broadcast_multiply_fusion
  9.9 0.6 reduce-window.6
  10.8 0.8 copy.34
  11.8 1.4 scatter_custom_fusion.2
  13.2 0.7 all_to_all.22
  13.9 8.3 %all-to-all-start.3 = ((f32[16,1,32]{2,1,0:T(1,128)}), f32[16,1,32]{2,1,0:T(1,128)S(1)}, u32[]{:S(2)}, u32[]{:S(2)}) async-start(f32[16,1,32]{2,1,0:T(1,128)} %all_to_all.22), calls=%async_computation.3 | async-start | bytes 16384 | tf_op jit(solution)/shard_map/all_to_all | solution.py:57
  22.2 1.9 gather_fusion
  24.1 1.3 scatter_custom_fusion.1
  25.6 0.7 reshape.227
  26.3 3.1 %all-to-all-done.3 = f32[16,1,32]{2,1,0:T(1,128)S(1)} async-done(((f32[16,1,32]{2,1,0:T(1,128)}), f32[16,1,32]{2,1,0:T(1,128)S(1)}, u32[]{:S(2)}, u32[]{:S(2)}) %all-to-all-start.3) | async-done | bytes 2080 | tf_op jit(solution)/shard_map/all_to_all | solution.py:57
  29.4 3.8 %all-to-all-start.1 = ((f32[16,1,128]{2,1,0:T(1,128)}), f32[16,1,128]{2,1,0:T(1,128)S(1)}, u32[]{:S(2)}, u32[]{:S(2)}) async-start(f32[16,1,128]{2,1,0:T(1,128)} %reshape.227), calls=%async_computation.1 | async-start | bytes 16384 | tf_op jit(solution)/shard_map/all_to_all | solution.py:58
  33.3 11.5 %scatter_custom_fusion = bf16[512,4096]{1,0:T(8,128)(2,1)} fusion(s32[256]{0:T(256)S(1)} %bitcast.121, bf16[128,4096]{1,0:T(8,128)(2,1)} %all-gather.3.cloned.1.call-done, s32[1024]{0:T(1024)S(1)} %pad_clamp_fusion.1, bf16[]{:T(256)} %constant.15.clone.1), kind=kCustom, calls=%fused_computation.39 | custom fusion | bytes 4194816 | tf_op jit(solution)/shard_map/scatter | solution.py:62
  44.7 7.1 %all-to-all-start = ((bf16[16,32,4096]{2,1,0:T(8,128)(2,1)}), bf16[16,32,4096]{2,1,0:T(8,128)(2,1)}, u32[]{:S(2)}, u32[]{:S(2)}) async-start(bf16[16,32,4096]{2,1,0:T(8,128)(2,1)} %bitcast.113), calls=%async_computation | async-start | bytes 8388608 | tf_op jit(solution)/shard_map/all_to_all | solution.py:63
  51.9 2.2 %all-gather = bf16[1,64,4096]{2,1,0:T(8,128)(2,1)S(1)} all-gather(bf16[1,64,2048]{2,1,0:T(8,128)(2,1)S(1)} %copy-done.2), channel_id=2, replica_groups=mesh['expert'=16,'tensor'=2] {'tensor'}, dimensions={2}, use_global_device_ids=true | all-gather | bytes 786432 | tf_op jit(solution)/shard_map/all_gather | solution.py:88
  54.7 0.7 reduce.9
  55.9 0.7 reduce.10
  56.8 3.2 %fusion.33 = f32[512,64]{0,1:T(8,128)} fusion(f32[512,64]{0,1:T(8,128)S(1)} %bitcast.115, bf16[1,512,1536]{2,1,0:T(8,128)(2,1)} %param.14, bf16[1,512,1536]{2,1,0:T(8,128)(2,1)S(1)} %copy-done.3, bf16[1,1536,64]{1,2,0:T(8,128)(2,1)S(1)} %copy-done), kind=kOutput, calls=%fused_computation.48 | convolution fusion | flops 106987520 | bytes 3604480 | tf_op jit(solution)/shard_map/dot_general | solution.py:84
  60.0 70.4 %all-to-all-done = bf16[16,32,4096]{2,1,0:T(8,128)(2,1)} async-done(((bf16[16,32,4096]{2,1,0:T(8,128)(2,1)}), bf16[16,32,4096]{2,1,0:T(8,128)(2,1)}, u32[]{:S(2)}, u32[]{:S(2)}) %all-to-all-start) | async-done | bytes 4194336 | tf_op jit(solution)/shard_map/all_to_all | solution.py:63
  130.4 12.2 %fusion = f32[512,1536]{1,0:T(8,128)} fusion(bf16[512,4096]{1,0:T(8,128)(2,1)} %bitcast.7, bf16[1,1536,4096]{2,1,0:T(8,128)(2,1)} %param.15), kind=kOutput, calls=%fused_computation.6 | convolution fusion | flops 6442450944 | bytes 19922944 | tf_op jit(solution)/shard_map/dot_general | solution.py:80
  142.6 3.7 %multiply_reduce_fusion.1 = (f32[512]{0:T(512)S(1)}, f32[512,64]{0,1:T(8,128)S(1)}) fusion(f32[512,64]{0,1:T(8,128)} %all-reduce.2.cloned.1.call-done, f32[512,64]{0,1:T(8,128)S(1)} %bitcast.116, bf16[512,4096]{1,0:T(8,128)(2,1)} %bitcast.7, bf16[1,64,4096]{2,1,0:T(8,128)(2,1)S(1)} %all-gather), kind=kOutput, calls=%fused_computation.54 | convolution fusion | flops 268533248 | bytes 5113856 | tf_op jit(solution)/shard_map/dot_general | solution.py:90
  146.3 1.9 fusion.20
  148.2 3.8 %fusion.28 = (bf16[1,512,1536]{2,1,0:T(8,128)(2,1)}, bf16[1,512,1536]{2,1,0:T(8,128)(2,1)}, f32[512]{0:T(512)S(1)}) fusion(bf16[1,512,1536]{2,1,0:T(8,128)(2,1)S(1)} %copy-done.3, bf16[1,512,1536]{2,1,0:T(8,128)(2,1)S(1)} %copy-done.4, f32[512,1536]{1,0:T(8,128)S(1)} %copy-done.5, bf16[1,1536,64]{1,2,0:T(8,128)(2,1)S(1)} %copy-done, ...), kind=kOutput, calls=%fused_computation.43 | convolution fusion | flops 117210624 | bytes 9768960 | tf_op jit(solution)/shard_map/dot_general | solution.py:96
  152.0 2.4 %psum.14 = f32[512]{0:T(512)S(1)} all-reduce(f32[512]{0:T(512)S(1)} %get-tuple-element.22), channel_id=1, replica_groups=mesh['expert'=16,'tensor'=2] {'tensor'}, use_global_device_ids=true, to_apply=%region_5.6 | all-reduce | flops 512 | bytes 4096 | tf_op jit(solution)/shard_map/psum | solution.py:95
  154.4 0.7 all_to_all.20
  155.1 18.7 %all-to-all-start.2 = ((f32[16,1,32]{2,1,0:T(1,128)}), f32[16,1,32]{2,1,0:T(1,128)S(1)}, u32[]{:S(2)}, u32[]{:S(2)}) async-start(f32[16,1,32]{2,1,0:T(1,128)} %all_to_all.20), calls=%async_computation.2 | async-start | bytes 16384 | tf_op jit(solution)/shard_map/all_to_all | solution.py:120
  173.8 2.9 %fusion.21 = f32[1,64,2048]{2,1,0:T(8,128)} fusion(bf16[512,4096]{1,0:T(8,128)(2,1)} %bitcast.7, s32[]{:T(128)S(6)} %select_n.46, f32[512,64]{0,1:T(8,128)S(1)} %copy-done.1, f32[512]{0:T(512)S(1)} %mul.123), kind=kOutput, calls=%fused_computation.37 | convolution fusion | flops 134414336 | bytes 2754564 | tf_op jit(solution)/shard_map/dot_general | solution.py:111
  176.7 4.4 %all-to-all-done.2 = f32[16,1,32]{2,1,0:T(1,128)S(1)} async-done(((f32[16,1,32]{2,1,0:T(1,128)}), f32[16,1,32]{2,1,0:T(1,128)S(1)}, u32[]{:S(2)}, u32[]{:S(2)}) %all-to-all-start.2) | async-done | bytes 2080 | tf_op jit(solution)/shard_map/all_to_all | solution.py:120
  181.1 0.7 reduce.8
  181.9 1.9 %gather_fusion.1 = f32[256]{0:T(256)S(1)} fusion(f32[512]{0:T(512)S(1)} %reshape.146, s32[1024]{0:T(1024)S(1)} %pad_clamp_fusion), kind=kCustom, calls=%fused_computation.2 | custom fusion | bytes 3072 | tf_op jit(solution)/shard_map/gather | solution.py:127
  184.0 0.6 copy.35
  (43 shorter events, 2.9 us)
Async XLA Ops:
  7.2 49.7 %copy-start = (bf16[1,1536,64]{1,2,0:T(8,128)(2,1)S(1)}, bf16[1,1536,64]{1,2,0:T(8,128)(2,1)}, u32[]{:S(2)}) copy-start(bf16[1,1536,64]{1,2,0:T(8,128)(2,1)} %param.16) | copy-start | bytes 589828
  7.2 26.1 %all-gather.3.cloned.1.call-start = ((), (), s32[]{:S(2)}) async-start(), calls=%async_computation.4 | async-start | bytes 1572864 | tf_op jit(solution)/shard_map/all_gather | solution.py:60
  13.9 15.5 %all-to-all-start.3 = ((f32[16,1,32]{2,1,0:T(1,128)}), f32[16,1,32]{2,1,0:T(1,128)S(1)}, u32[]{:S(2)}, u32[]{:S(2)}) async-start(f32[16,1,32]{2,1,0:T(1,128)} %all_to_all.22), calls=%async_computation.3 | async-start | bytes 16384 | tf_op jit(solution)/shard_map/all_to_all | solution.py:57
  29.4 15.3 %all-to-all-start.1 = ((f32[16,1,128]{2,1,0:T(1,128)}), f32[16,1,128]{2,1,0:T(1,128)S(1)}, u32[]{:S(2)}, u32[]{:S(2)}) async-start(f32[16,1,128]{2,1,0:T(1,128)} %reshape.227), calls=%async_computation.1 | async-start | bytes 16384 | tf_op jit(solution)/shard_map/all_to_all | solution.py:58
  44.7 7.2 %copy-start.2 = (bf16[1,64,2048]{2,1,0:T(8,128)(2,1)S(1)}, bf16[1,64,2048]{2,1,0:T(8,128)(2,1)}, u32[]{:S(2)}) copy-start(bf16[1,64,2048]{2,1,0:T(8,128)(2,1)} %param.17) | copy-start | bytes 786436
  44.7 12.1 %copy-start.3 = (bf16[1,512,1536]{2,1,0:T(8,128)(2,1)S(1)}, bf16[1,512,1536]{2,1,0:T(8,128)(2,1)}, u32[]{:S(2)}) copy-start(bf16[1,512,1536]{2,1,0:T(8,128)(2,1)} %param.13) | copy-start | bytes 4718596
  44.7 85.7 %all-to-all-start = ((bf16[16,32,4096]{2,1,0:T(8,128)(2,1)}), bf16[16,32,4096]{2,1,0:T(8,128)(2,1)}, u32[]{:S(2)}, u32[]{:S(2)}) async-start(bf16[16,32,4096]{2,1,0:T(8,128)(2,1)} %bitcast.113), calls=%async_computation | async-start | bytes 8388608 | tf_op jit(solution)/shard_map/all_to_all | solution.py:63
  51.8 90.8 %all-reduce.2.cloned.1.call-start = ((), (), s32[]{:S(2)}) async-start(), calls=%async_computation.5 | async-start | bytes 262144 | tf_op jit(solution)/shard_map/psum | solution.py:95
  142.6 3.7 %copy-start.4 = (bf16[1,512,1536]{2,1,0:T(8,128)(2,1)S(1)}, bf16[1,512,1536]{2,1,0:T(8,128)(2,1)}, u32[]{:S(2)}) copy-start(bf16[1,512,1536]{2,1,0:T(8,128)(2,1)} %param.14) | copy-start | bytes 4718596
  146.3 1.9 copy-start.5
  148.2 25.6 %copy-start.1 = (f32[512,64]{0,1:T(8,128)S(1)}, f32[512,64]{0,1:T(8,128)}, u32[]{:S(2)}) copy-start(f32[512,64]{0,1:T(8,128)} %all-reduce.2.cloned.1.call-done) | copy-start | bytes 393220
  155.1 26.0 %all-to-all-start.2 = ((f32[16,1,32]{2,1,0:T(1,128)}), f32[16,1,32]{2,1,0:T(1,128)S(1)}, u32[]{:S(2)}, u32[]{:S(2)}) async-start(f32[16,1,32]{2,1,0:T(1,128)} %all_to_all.20), calls=%async_computation.2 | async-start | bytes 16384 | tf_op jit(solution)/shard_map/all_to_all | solution.py:120
Sparse Core Ops, SparseCore 0:
  9.6 11.7 all-gather.2
  60.1 19.1 all-reduce.1
where the time goes:
time: 192 us; the launch traced here: 191 us
  waiting for transfers between devices  78.6 us (41%)
  starting transfers between devices  38 us (20%)
  matrix products  27.6 us (14%)
  local copies, waits for them, and re-layouts  23.6 us (12%)
  between operations  14.3 us (7%)
  other arithmetic  4.82 us (3%)
  blocking collectives  4.63 us (2%)
    all_to_all x1, waiting for transfers between devices, local(): lax.all_to_all(buffer.reshape(experts, per_source, full_width), 'expert',...  70.4 us
    all_to_all x1, starting transfers between devices, local(): lax.all_to_all(slot_gradient.reshape(experts, per_source), 'expert', spli...  18.7 us
    dot_general x1, matrix products, local(): lax.dot_general(token_rows, down_matrix[0], contract_dims, preferred_elem...  12.2 us
    scatter x1, local copies, waits for them, and re-layouts, local(): jnp.zeros((experts * per_source, full_width), whole.dtype).at[slot]  11.5 us
    all_to_all x1, starting transfers between devices, local(): lax.all_to_all(weight_slots, 'expert', split_axis=0, concat_axis=0, tiled...  8.31 us
    all_to_all x1, starting transfers between devices, local(): lax.all_to_all(buffer.reshape(experts, per_source, full_width), 'expert',...  7.09 us
    all_to_all x1, waiting for transfers between devices, local(): lax.all_to_all(slot_gradient.reshape(experts, per_source), 'expert', spli...  4.39 us
  transfers between devices with their start and end apart: 6, of which 3 were waited for; matrix products, arithmetic and copies ran while one was open for 22% of the time, Pallas kernels for 0%

commit v1 on v0

--- a/solution.py
+++ b/solution.py
@@ -1,3 +1,5 @@
+import functools
+
 import jax
 import jax.numpy as jnp
 from jax import lax
@@ -32,45 +34,46 @@
     slots = gate_preactivation.shape[1]
     per_source = slots // experts
     adapter_groups = adapter_input_maps.shape[2] // ADAPTER_RANK
-    picks = routes.reshape(-1)
-    onehot = (picks[:, None] == jnp.arange(experts, dtype=jnp.int32)).astype(jnp.int32)
-    before = jnp.cumsum(onehot, axis=0) - onehot
-    rank = jnp.sum(before * onehot, axis=1)
-    slot = picks * per_source + rank
-    owner = jnp.arange(tok_rows * picks_per, dtype=jnp.int32) // picks_per
-    weight_slots = (
-        jnp.zeros((experts * per_source,), jnp.float32)
-        .at[slot]
-        .set(router_weight.reshape(-1))
-        .reshape(experts, per_source)
+    token_ids = jnp.arange(tok_rows, dtype=jnp.int32)
+    expert_ids = jnp.arange(experts, dtype=jnp.int32)
+    slot_ids = jnp.arange(experts * per_source, dtype=jnp.int32)
+    hits = (routes[:, :, None] == expert_ids).astype(jnp.float32)
+    earlier = (token_ids[:, None] > token_ids[None, :]).astype(jnp.bfloat16)
+    before = jnp.dot(
+        earlier, jnp.sum(hits, axis=1).astype(jnp.bfloat16), preferred_element_type=jnp.float32
     )
-    client_hot = (clients[owner][:, None] == jnp.arange(adapter_groups, dtype=jnp.int32)).astype(
-        jnp.float32
+    rank = jnp.sum(before[:, None, :] * hits, axis=2).astype(jnp.int32)
+    slot = routes * per_source + rank
+    chosen = [slot_ids[:, None] == slot[None, :, k] for k in range(picks_per)]
+    filled = functools.reduce(jnp.logical_or, chosen)
+    weight_slots = sum(
+        jnp.sum(jnp.where(chosen[k], router_weight[None, :, k], 0.0), axis=1)
+        for k in range(picks_per)
     )
-    chosen_slots = (
-        jnp.zeros((experts * per_source, adapter_groups), jnp.float32)
-        .at[slot]
-        .set(client_hot)
-        .reshape(experts, per_source, adapter_groups)
+    client_slots = jnp.sum(
+        jnp.where(filled, (clients[None, :] + 1).astype(jnp.float32), 0.0), axis=1
     )
-    weight_in, chosen_in = (
-        lax.all_to_all(weight_slots, "expert", split_axis=0, concat_axis=0, tiled=True),
-        lax.all_to_all(chosen_slots, "expert", split_axis=0, concat_axis=0, tiled=True),
+    facts = jnp.concatenate(
+        [weight_slots.reshape(experts, per_source), client_slots.reshape(experts, per_source)],
+        axis=1,
     )
-    whole = lax.all_gather(cotangent, "tensor", axis=1, tiled=True)
-    full_width = whole.shape[1]
-    buffer = jnp.zeros((experts * per_source, full_width), whole.dtype).at[slot].set(whole[owner])
-    arrived = lax.all_to_all(
-        buffer.reshape(experts, per_source, full_width),
+    facts_in = lax.all_to_all(facts, "expert", split_axis=0, concat_axis=0, tiled=True)
+    buffer = jnp.dot(
+        filled.astype(jnp.bfloat16), cotangent, preferred_element_type=jnp.float32
+    ).astype(cotangent.dtype)
+    part = lax.all_to_all(
+        buffer.reshape(experts, per_source, width),
         "expert",
         split_axis=0,
         concat_axis=0,
         tiled=True,
-    )
-    token_rows = arrived.reshape(slots, full_width)
-    part = lax.dynamic_slice_in_dim(token_rows, lax.axis_index("tensor") * width, width, 1)
-    pick_weight = weight_in.reshape(slots)
-    client_mask = jnp.repeat(chosen_in.reshape(slots, adapter_groups), ADAPTER_RANK, axis=1)
+    ).reshape(slots, width)
+    token_rows = lax.all_gather(part, "tensor", axis=1, tiled=True)
+    pick_weight = facts_in[:, :per_source].reshape(slots)
+    column_client = jnp.arange(adapter_groups * ADAPTER_RANK, dtype=jnp.int32) // ADAPTER_RANK
+    client_mask = (
+        facts_in[:, per_source:].reshape(slots, 1) == (column_client + 1).astype(jnp.float32)
+    ).astype(jnp.float32)
     act, slope = silu_parts(gate_preactivation[0].astype(jnp.float32))
     up_full = up_preactivation[0].astype(jnp.float32)
     hidden_units = act * up_full
@@ -92,7 +95,7 @@
         )
         * client_mask
     )
-    projected_rows, router_products = lax.psum((projected_piece, local_terms), "tensor")
+    projected_rows = lax.psum(projected_piece, "tensor")
     backward_result = lax.dot_general(
         adapter_output.astype(jnp.bfloat16),
         adapter_input_maps[0],
@@ -114,17 +117,22 @@
         row_dimensions,
         preferred_element_type=jnp.float32,
     )
-    slot_gradient = router_products + adapter_scale * jnp.sum(
-        projected_rows * adapter_output, axis=1
+    slot_piece = local_terms + adapter_scale * jnp.sum(projected_piece * adapter_output, axis=1)
+    tensors = lax.axis_size("tensor")
+    outgoing = jnp.broadcast_to(
+        slot_piece.reshape(experts, 1, per_source), (experts, tensors, per_source)
+    ).reshape(experts * tensors, per_source)
+    returned = lax.all_to_all(
+        outgoing, ("expert", "tensor"), split_axis=0, concat_axis=0, tiled=True
     )
-    returned = lax.all_to_all(
-        slot_gradient.reshape(experts, per_source),
-        "expert",
-        split_axis=0,
-        concat_axis=0,
-        tiled=True,
+    slot_gradient = jnp.sum(returned.reshape(experts, tensors, per_source), axis=1).reshape(-1)
+    gate_grad = jnp.stack(
+        [
+            jnp.sum(jnp.where(chosen[k], slot_gradient[:, None], 0.0), axis=0)
+            for k in range(picks_per)
+        ],
+        axis=1,
     )
-    gate_grad = returned.reshape(-1)[slot].reshape(tok_rows, picks_per)
     return (
         gate_grad,
         gate_gradient[None],

time: 192 us -> 139 us (0.72)
  waiting for transfers between devices: 78.6 us -> 23.5 us
  blocking collectives: 4.63 us -> 59.4 us
  starting transfers between devices: 38 us -> 9.32 us
  local copies, waits for them, and re-layouts: 23.6 us -> 1.2 us
    all_to_all x4 -> x2, waiting for transfers between devices: 77.8 us -> 8.16 us  [the longest x1 5 us: local(): lax.all_to_all(facts, 'expert', split_axis=0, concat_axis=0, tiled=True)]
    all_to_all x0 -> x1, blocking collectives: none -> 57.2 us  [local(): lax.all_to_all(buffer.reshape(experts, per_source, width), 'expert', spli...]
    all_to_all x4 -> x2, starting transfers between devices: 37.9 us -> 9.24 us  [the longest x1 5.34 us: local(): lax.all_to_all(outgoing, ('expert', 'tensor'), split_axis=0, concat_axis=...]
    psum x1, waiting for transfers between devices: 0.01 us -> 15.3 us  [local(): projected_rows = lax.psum(projected_piece, 'tensor')]
    scatter x2 -> x0, local copies, waits for them, and re-layouts: 12.9 us -> none  [the longest x1 11.5 us: local(): jnp.zeros((experts * per_source, full_width), whole.dtype).at[slot]]
    gather x2 -> x0, local copies, waits for them, and re-layouts: 3.84 us -> none  [the longest x1 1.94 us: local(): gate_grad = returned.reshape(-1)[slot].reshape(tok_rows, picks_per)]
    unnamed x17 -> x18, local copies, waits for them, and re-layouts: 3.03 us -> 0.05 us
    dot_general x1, matrix products: 12.2 us -> 9.48 us  [local(): lax.dot_general(token_rows, down_matrix[0], contract_dims, preferred_elem...]
  transfers between devices with their start and end apart: 6 -> 4, of which waited for: 3 -> 3; matrix products, arithmetic and copies ran while one was open for 22% -> 4% of each run, Pallas kernels for 0% -> 0%
where the time goes in v1:
time: 139 us
  blocking collectives  59.4 us (43%)
  matrix products  27.6 us (20%)
  waiting for transfers between devices  23.5 us (17%)
  between operations  14.2 us (10%)
  starting transfers between devices  9.32 us (7%)
  other arithmetic  3.88 us (3%)
    all_to_all x1, blocking collectives, local(): lax.all_to_all(buffer.reshape(experts, per_source, width), 'expert', spli...  57.2 us
    psum x1, waiting for transfers between devices, local(): projected_rows = lax.psum(projected_piece, 'tensor')  15.3 us
    dot_general x1, matrix products, local(): lax.dot_general(token_rows, down_matrix[0], contract_dims, preferred_elem...  9.48 us
    all_to_all x1, starting transfers between devices, local(): lax.all_to_all(outgoing, ('expert', 'tensor'), split_axis=0, concat_axis=...  5.34 us
    all_to_all x1, waiting for transfers between devices, local(): lax.all_to_all(facts, 'expert', split_axis=0, concat_axis=0, tiled=True)  5 us
    dot_general x1, matrix products, local(): lax.dot_general(hidden_lowrank, (pick_weight[:, None] * adapter_output).a...  3.91 us
    all_to_all x1, starting transfers between devices, local(): lax.all_to_all(facts, 'expert', split_axis=0, concat_axis=0, tiled=True)  3.89 us
    dot_general x1, matrix products, local(): jnp.dot(hidden_lowrank, adapter_input_maps[0], preferred_element_type=jnp...  3.79 us
  transfers between devices with their start and end apart: 4, of which 3 were waited for; matrix products, arithmetic and copies ran while one was open for 4% of the time, Pallas kernels for 0%

profile of v1, /device:TPU:0, one launch (start us, length us, event | category | flops | bytes accessed | tf_op | source)
XLA Modules:
  0.0 139.0 jit_solution(5740434610580496316)
XLA Ops:
  7.2 0.0 all-gather.3.cloned.1.call-start
  7.2 0.7 convert_reduce_fusion
  8.0 0.1 fusion.42
  8.1 0.7 select_reduce_fusion.5
  8.8 0.7 convert_add_fusion
  9.5 0.7 convolution_convert_fusion
  10.2 57.2 %all_to_all.26 = bf16[16,32,2048]{2,1,0:T(8,128)(2,1)} all-to-all(bf16[16,32,2048]{2,1,0:T(8,128)(2,1)S(1)} %bitcast.103), channel_id=1, replica_groups=mesh['expert'=16,'tensor'=2] {'expert'}, dimensions={0} | all-to-all | bytes 4194304 | tf_op jit(solution)/shard_map/all_to_all | solution.py:64
  67.5 0.3 select_reduce_fusion.3
  67.8 0.1 add.57
  67.9 0.1 reshape.82
  68.0 0.7 pad_maximum_fusion
  68.7 3.9 %all-to-all-start.1 = ((f32[16,1,64]{2,1,0:T(1,128)}), f32[16,1,64]{2,1,0:T(1,128)S(1)}, u32[]{:S(2)}, u32[]{:S(2)}) async-start(f32[16,1,64]{2,1,0:T(1,128)} %bitcast.9), calls=%async_computation.1 | async-start | bytes 16384 | tf_op jit(solution)/shard_map/all_to_all | solution.py:60
  72.6 2.2 %all-gather = bf16[1,64,4096]{2,1,0:T(8,128)(2,1)S(1)} all-gather(bf16[1,64,2048]{2,1,0:T(8,128)(2,1)S(1)} %copy-done.3), channel_id=2, replica_groups=mesh['expert'=16,'tensor'=2] {'tensor'}, dimensions={2}, use_global_device_ids=true | all-gather | bytes 786432 | tf_op jit(solution)/shard_map/all_gather | solution.py:91
  74.8 5.0 %all-to-all-done.1 = f32[16,1,64]{2,1,0:T(1,128)S(1)} async-done(((f32[16,1,64]{2,1,0:T(1,128)}), f32[16,1,64]{2,1,0:T(1,128)S(1)}, u32[]{:S(2)}, u32[]{:S(2)}) %all-to-all-start.1) | async-done | bytes 4128 | tf_op jit(solution)/shard_map/all_to_all | solution.py:60
  79.8 0.1 fusion.48
  79.8 0.1 mul.120
  79.9 0.1 eq.69
  80.0 3.6 %convolution_select_fusion = f32[512,64]{0,1:T(8,128)S(1)} fusion(bf16[512,4096]{1,0:T(8,128)(2,1)} %all-gather.3.cloned.1.call-done, bf16[1,64,4096]{2,1,0:T(8,128)(2,1)S(1)} %all-gather, f32[512]{0:T(512)S(1)} %eq.69, f32[64]{0:T(128)S(1)} %fusion.45), kind=kOutput, calls=%fused_computation.38 | convolution fusion | flops 268500992 | bytes 4851968 | tf_op jit(solution)/shard_map/dot_general | solution.py:93
  83.6 3.8 %multiply_reduce_fusion.1 = (f32[512]{0:T(512)S(1)}, f32[512,64]{0,1:T(8,128)}) fusion(f32[512,64]{0,1:T(8,128)S(1)} %convolution_select_fusion, bf16[1,1536,64]{1,2,0:T(8,128)(2,1)S(1)} %copy-done.7, bf16[1,512,1536]{2,1,0:T(8,128)(2,1)} %param.14, bf16[1,512,1536]{2,1,0:T(8,128)(2,1)} %param.13, f32[64]{0:T(128)S(1)} %fusion.45, f32[512]{0:T(512)S(1)} %eq.69), kind=kOutput, calls=%fused_computation.53 | convolution fusion | flops 107085312 | bytes 3608832 | tf_op jit(solution)/shard_map/dot_general | solution.py:87
  87.4 9.5 %fusion = f32[512,1536]{1,0:T(8,128)S(1)} fusion(bf16[512,4096]{1,0:T(8,128)(2,1)S(1)} %copy-done.2, bf16[1,1536,4096]{2,1,0:T(8,128)(2,1)} %param.15), kind=kOutput, calls=%fused_computation | convolution fusion | flops 6442450944 | bytes 19922944 | tf_op jit(solution)/shard_map/dot_general | solution.py:83
  96.9 3.8 %fusion.24 = (bf16[1,512,1536]{2,1,0:T(8,128)(2,1)}, bf16[1,512,1536]{2,1,0:T(8,128)(2,1)}, f32[512]{0:T(512)S(1)}) fusion(bf16[1,512,1536]{2,1,0:T(8,128)(2,1)S(1)} %copy-done.5, bf16[1,512,1536]{2,1,0:T(8,128)(2,1)S(1)} %copy-done.6, f32[512,1536]{1,0:T(8,128)S(1)} %fusion, bf16[1,1536,64]{1,2,0:T(8,128)(2,1)S(1)} %copy-done.7, ...), kind=kOutput, calls=%fused_computation.34 | convolution fusion | flops 117210624 | bytes 9768960 | tf_op jit(solution)/shard_map/dot_general | solution.py:99
  100.7 0.1 add.63
  100.8 0.6 broadcast_in_dim.76
  101.4 5.3 %all-to-all-start.2 = ((f32[32,1,32]{2,1,0:T(1,128)}), f32[32,1,32]{2,1,0:T(1,128)S(1)}, u32[]{:S(2)}, u32[]{:S(2)}) async-start(f32[32,1,32]{2,1,0:T(1,128)} %bitcast.14), calls=%async_computation.2 | async-start | bytes 32768 | tf_op jit(solution)/shard_map/all_to_all | solution.py:125
  106.7 0.0 all-reduce.2.cloned.1.call-start
  106.8 3.9 %fusion.20 = f32[1,1536,64]{1,2,0:T(8,128)} fusion(bf16[1,512,1536]{2,1,0:T(8,128)(2,1)} %param.14, f32[512,64]{0,1:T(8,128)S(1)} %convolution_select_fusion, f32[512]{0:T(512)S(1)} %mul.120, bf16[1,512,1536]{2,1,0:T(8,128)(2,1)} %param.13), kind=kOutput, calls=%fused_computation.30 | convolution fusion | flops 107118592 | bytes 3672064 | tf_op jit(solution)/shard_map/dot_general | solution.py:108
  110.7 3.2 %all-to-all-done.2 = f32[32,1,32]{2,1,0:T(1,128)S(1)} async-done(((f32[32,1,32]{2,1,0:T(1,128)}), f32[32,1,32]{2,1,0:T(1,128)S(1)}, u32[]{:S(2)}, u32[]{:S(2)}) %all-to-all-start.2) | async-done | bytes 4128 | tf_op jit(solution)/shard_map/all_to_all | solution.py:125
  113.9 0.1 broadcast_in_dim.77
  114.0 0.2 select_reduce_fusion.1
  114.1 0.6 pad_maximum_fusion.1
  114.7 15.3 %all-reduce.2.cloned.1.call-done = f32[512,64]{0,1:T(8,128)} async-done(((f32[512,64]{0,1:T(8,128)}), f32[512,64]{0,1:T(8,128)}) %all-reduce.2.cloned.1.call-update) | async-done | bytes 131088 | tf_op jit(solution)/shard_map/psum | solution.py:98
  130.0 2.2 %fusion.21 = f32[1,64,2048]{2,1,0:T(8,128)} fusion(bf16[512,2048]{1,0:T(8,128)(2,1)S(1)} %bitcast.102, f32[512,64]{0,1:T(8,128)} %all-reduce.2.cloned.1.call-done, f32[512]{0:T(512)S(1)} %mul.120), kind=kOutput, calls=%fused_computation.32 | convolution fusion | flops 134414336 | bytes 2754560 | tf_op jit(solution)/shard_map/dot_general | solution.py:114
  (28 shorter events, 0.1 us)
Async XLA Ops:
  7.2 2.3 %copy-start = (bf16[128,2048]{1,0:T(8,128)(2,1)S(1)}, bf16[128,2048]{1,0:T(8,128)(2,1)}, u32[]{:S(2)}) copy-start(bf16[128,2048]{1,0:T(8,128)(2,1)} %param.9) | copy-start | bytes 1572868
  7.2 72.8 %all-gather.3.cloned.1.call-start = ((), (), s32[]{:S(2)}) async-start(), calls=%async_computation.3 | async-start | bytes 6291456 | tf_op jit(solution)/shard_map/all_gather | solution.py:71
  10.2 57.3 %copy-start.8 = (s32[128]{0:T(128)S(1)}, s32[128]{0:T(128)}, u32[]{:S(2)}) copy-start(s32[128]{0:T(128)} %param.12) | copy-start | bytes 1540
  10.2 57.3 %copy-start.4 = (f32[128,2]{0,1:T(2,128)S(1)}, f32[128,2]{0,1:T(2,128)}, u32[]{:S(2)}) copy-start(f32[128,2]{0,1:T(2,128)} %param.11) | copy-start | bytes 3076
  10.2 62.3 %copy-start.3 = (bf16[1,64,2048]{2,1,0:T(8,128)(2,1)S(1)}, bf16[1,64,2048]{2,1,0:T(8,128)(2,1)}, u32[]{:S(2)}) copy-start(bf16[1,64,2048]{2,1,0:T(8,128)(2,1)} %param.17) | copy-start | bytes 786436
  67.5 16.1 %copy-start.7 = (bf16[1,1536,64]{1,2,0:T(8,128)(2,1)S(1)}, bf16[1,1536,64]{1,2,0:T(8,128)(2,1)}, u32[]{:S(2)}) copy-start(bf16[1,1536,64]{1,2,0:T(8,128)(2,1)} %param.16) | copy-start | bytes 589828
  68.7 11.1 %all-to-all-start.1 = ((f32[16,1,64]{2,1,0:T(1,128)}), f32[16,1,64]{2,1,0:T(1,128)S(1)}, u32[]{:S(2)}, u32[]{:S(2)}) async-start(f32[16,1,64]{2,1,0:T(1,128)} %bitcast.9), calls=%async_computation.1 | async-start | bytes 16384 | tf_op jit(solution)/shard_map/all_to_all | solution.py:60
  83.6 3.8 %copy-start.2 = (bf16[512,4096]{1,0:T(8,128)(2,1)S(1)}, bf16[512,4096]{1,0:T(8,128)(2,1)}, u32[]{:S(2)}) copy-start(bf16[512,4096]{1,0:T(8,128)(2,1)} %all-gather.3.cloned.1.call-done) | copy-start | bytes 12582916
  87.4 9.5 %copy-start.5 = (bf16[1,512,1536]{2,1,0:T(8,128)(2,1)S(1)}, bf16[1,512,1536]{2,1,0:T(8,128)(2,1)}, u32[]{:S(2)}) copy-start(bf16[1,512,1536]{2,1,0:T(8,128)(2,1)} %param.13) | copy-start | bytes 4718596
  87.4 9.5 %copy-start.6 = (bf16[1,512,1536]{2,1,0:T(8,128)(2,1)S(1)}, bf16[1,512,1536]{2,1,0:T(8,128)(2,1)}, u32[]{:S(2)}) copy-start(bf16[1,512,1536]{2,1,0:T(8,128)(2,1)} %param.14) | copy-start | bytes 4718596
  101.4 12.5 %all-to-all-start.2 = ((f32[32,1,32]{2,1,0:T(1,128)}), f32[32,1,32]{2,1,0:T(1,128)S(1)}, u32[]{:S(2)}, u32[]{:S(2)}) async-start(f32[32,1,32]{2,1,0:T(1,128)} %bitcast.14), calls=%async_computation.2 | async-start | bytes 32768 | tf_op jit(solution)/shard_map/all_to_all | solution.py:125
  106.7 23.3 %copy-start.1 = (bf16[16,32,2048]{2,1,0:T(8,128)(2,1)S(1)}, bf16[16,32,2048]{2,1,0:T(8,128)(2,1)}, u32[]{:S(2)}) copy-start(bf16[16,32,2048]{2,1,0:T(8,128)(2,1)} %all_to_all.26) | copy-start | bytes 6291460
  106.7 23.3 %all-reduce.2.cloned.1.call-start = ((), (), s32[]{:S(2)}) async-start(), calls=%async_computation.4 | async-start | bytes 262144 | tf_op jit(solution)/shard_map/psum | solution.py:98
Sparse Core Ops, SparseCore 0:
  67.6 11.9 all-gather.2
  110.8 19.1 all-reduce.1

commit v2 on v1

--- a/solution.py
+++ b/solution.py
@@ -3,12 +3,167 @@
 import jax
 import jax.numpy as jnp
 from jax import lax
+from jax.experimental import pallas as pl
+from jax.experimental.pallas import tpu as pltpu
 from jax.sharding import PartitionSpec as P
 
 ADAPTER_RANK = 16
 
 
 adapter_scale = 2.0
+
+
+MESH = pl.DeviceIdType.MESH
+TILE_ROWS = 16
+LANES = 128
+
+
+def exchange_kernel(
+    experts,
+    blocks,
+    facts,
+    piece,
+    maps,
+    rows,
+    facts_in,
+    other_piece,
+    maps_whole,
+    row_send,
+    row_recv,
+    fact_send,
+    fact_recv,
+    pass_send,
+    pass_recv,
+    pair_send,
+    pair_recv,
+    own_sem,
+):
+    expert = lax.axis_index("expert")
+    tensor = lax.axis_index("tensor")
+    width = blocks.shape[2]
+    columns = pl.ds(pl.multiple_of(tensor * width, LANES), width)
+    partner = (expert, 1 - tensor)
+
+    barrier = pltpu.get_barrier_semaphore()
+
+    @pl.loop(1, experts)
+    def _(step):
+        peer = lax.rem(expert + step, experts)
+        pl.semaphore_signal(barrier, inc=1, device_id=(peer, tensor), device_id_type=MESH)
+
+    pl.semaphore_signal(barrier, inc=1, device_id=partner, device_id_type=MESH)
+    pl.semaphore_wait(barrier, experts)
+
+    def remote(source, target, send, recv, device):
+        return pltpu.make_async_remote_copy(
+            src_ref=source,
+            dst_ref=target,
+            send_sem=send,
+            recv_sem=recv,
+            device_id=device,
+            device_id_type=MESH,
+        )
+
+    def row_copy(step):
+        peer = lax.rem(expert + step, experts)
+        return remote(
+            blocks.at[peer],
+            rows.at[expert, :, columns],
+            row_send.at[step],
+            row_recv.at[step],
+            (peer, tensor),
+        )
+
+    def fact_copy(step):
+        peer = lax.rem(expert + step, experts)
+        return remote(
+            facts.at[peer],
+            facts_in.at[expert],
+            fact_send.at[step],
+            fact_recv.at[step],
+            (peer, tensor),
+        )
+
+    def pass_copy(step):
+        source = lax.rem(expert - step + experts, experts)
+        return remote(
+            rows.at[source, :, columns],
+            rows.at[source, :, columns],
+            pass_send.at[step],
+            pass_recv.at[step],
+            partner,
+        )
+
+    @pl.loop(1, experts)
+    def _(step):
+        row_copy(step).start()
+
+    @pl.loop(1, experts)
+    def _(step):
+        fact_copy(step).start()
+
+    own_copies = [
+        pltpu.make_async_copy(blocks.at[expert], rows.at[expert, :, columns], own_sem.at[0]),
+        pltpu.make_async_copy(facts.at[expert], facts_in.at[expert], own_sem.at[1]),
+        pltpu.make_async_copy(maps, maps_whole.at[:, columns], own_sem.at[2]),
+    ]
+    pair_copies = [
+        remote(piece, other_piece, pair_send.at[0], pair_recv.at[0], partner),
+        remote(maps, maps_whole.at[:, columns], pair_send.at[1], pair_recv.at[1], partner),
+        remote(
+            blocks.at[expert],
+            rows.at[expert, :, columns],
+            pair_send.at[2],
+            pair_recv.at[2],
+            partner,
+        ),
+    ]
+    for copy in own_copies + pair_copies:
+        copy.start()
+
+    @pl.loop(1, experts)
+    def _(step):
+        row_copy(step).wait_recv()
+        pass_copy(step).start()
+
+    for copy in own_copies + pair_copies:
+        copy.wait()
+
+    @pl.loop(1, experts)
+    def _(step):
+        fact_copy(step).wait()
+        row_copy(step).wait_send()
+        pass_copy(step).wait()
+
+
+def exchange(blocks, facts, piece, maps):
+    experts, per_source, width = blocks.shape
+    anywhere = pl.BlockSpec(memory_space=pl.ANY)
+    sems = pltpu.SemaphoreType.DMA
+    return pl.pallas_call(
+        functools.partial(exchange_kernel, experts),
+        out_shape=(
+            jax.ShapeDtypeStruct((experts, per_source, 2 * width), blocks.dtype),
+            jax.ShapeDtypeStruct(facts.shape, facts.dtype),
+            jax.ShapeDtypeStruct(piece.shape, piece.dtype),
+            jax.ShapeDtypeStruct((maps.shape[0], 2 * width), maps.dtype),
+        ),
+        in_specs=[anywhere] * 4,
+        out_specs=(anywhere,) * 4,
+        scratch_shapes=[sems((experts,))] * 6 + [sems((3,))] * 3,
+        compiler_params=pltpu.CompilerParams(collective_id=0, has_side_effects=True),
+        name="exchange",
+    )(blocks, facts, piece, maps)
+
+
+def fits_exchange(experts, per_source, width):
+    return (
+        lax.axis_size("tensor") == 2
+        and per_source % TILE_ROWS == 0
+        and 2 * per_source <= LANES
+        and width % LANES == 0
+        and experts > 1
+    )
 
 
 def silu_parts(gate):
@@ -57,45 +212,54 @@
         [weight_slots.reshape(experts, per_source), client_slots.reshape(experts, per_source)],
         axis=1,
     )
-    facts_in = lax.all_to_all(facts, "expert", split_axis=0, concat_axis=0, tiled=True)
     buffer = jnp.dot(
         filled.astype(jnp.bfloat16), cotangent, preferred_element_type=jnp.float32
     ).astype(cotangent.dtype)
-    part = lax.all_to_all(
-        buffer.reshape(experts, per_source, width),
-        "expert",
-        split_axis=0,
-        concat_axis=0,
-        tiled=True,
-    ).reshape(slots, width)
-    token_rows = lax.all_gather(part, "tensor", axis=1, tiled=True)
-    pick_weight = facts_in[:, :per_source].reshape(slots)
-    column_client = jnp.arange(adapter_groups * ADAPTER_RANK, dtype=jnp.int32) // ADAPTER_RANK
-    client_mask = (
-        facts_in[:, per_source:].reshape(slots, 1) == (column_client + 1).astype(jnp.float32)
-    ).astype(jnp.float32)
     act, slope = silu_parts(gate_preactivation[0].astype(jnp.float32))
     up_full = up_preactivation[0].astype(jnp.float32)
     hidden_units = act * up_full
     hidden_lowrank = hidden_units.astype(jnp.bfloat16)
     contract_dims = (((1,), (1,)), ((), ()))
     row_dimensions = (((0,), (0,)), ((), ()))
+    unmasked_piece = jnp.dot(
+        hidden_lowrank, adapter_input_maps[0], preferred_element_type=jnp.float32
+    )
+    blocks = buffer.reshape(experts, per_source, width)
+    if fits_exchange(experts, per_source, width):
+        tiles = jnp.zeros((experts, 8, LANES), jnp.float32)
+        tiles = lax.dynamic_update_slice(tiles, facts[:, None, :], (0, 0, 0))
+        arrived, tiles_in, other_piece, output_map_whole = exchange(
+            blocks, tiles, unmasked_piece, adapter_output_maps[0]
+        )
+        facts_in = tiles_in[:, 0, : 2 * per_source]
+        token_rows = arrived.reshape(slots, 2 * width)
+        part = lax.dynamic_slice_in_dim(token_rows, lax.axis_index("tensor") * width, width, 1)
+        unmasked_rows = unmasked_piece + other_piece
+    else:
+        facts_in = lax.all_to_all(facts, "expert", split_axis=0, concat_axis=0, tiled=True)
+        part = lax.all_to_all(
+            blocks, "expert", split_axis=0, concat_axis=0, tiled=True
+        ).reshape(slots, width)
+        token_rows = lax.all_gather(part, "tensor", axis=1, tiled=True)
+        output_map_whole = lax.all_gather(adapter_output_maps[0], "tensor", axis=1, tiled=True)
+        unmasked_rows = lax.psum(unmasked_piece, "tensor")
+    pick_weight = facts_in[:, :per_source].reshape(slots)
+    column_client = jnp.arange(adapter_groups * ADAPTER_RANK, dtype=jnp.int32) // ADAPTER_RANK
+    client_mask = (
+        facts_in[:, per_source:].reshape(slots, 1) == (column_client + 1).astype(jnp.float32)
+    ).astype(jnp.float32)
     frozen_output = lax.dot_general(
         token_rows, down_matrix[0], contract_dims, preferred_element_type=jnp.float32
     )
-    projected_piece = (
-        jnp.dot(hidden_lowrank, adapter_input_maps[0], preferred_element_type=jnp.float32)
-        * client_mask
-    )
+    projected_piece = unmasked_piece * client_mask
+    projected_rows = unmasked_rows * client_mask
     local_terms = jnp.sum(hidden_units * frozen_output, axis=1)
-    output_map_whole = lax.all_gather(adapter_output_maps[0], "tensor", axis=1, tiled=True)
     adapter_output = (
         lax.dot_general(
             token_rows, output_map_whole, contract_dims, preferred_element_type=jnp.float32
         )
         * client_mask
     )
-    projected_rows = lax.psum(projected_piece, "tensor")
     backward_result = lax.dot_general(
         adapter_output.astype(jnp.bfloat16),
         adapter_input_maps[0],

time: 139 us -> 101 us (0.73)
  blocking collectives: 59.4 us -> 0 us
  Pallas kernels: 0 us -> 58.9 us
  waiting for transfers between devices: 23.5 us -> 0.72 us
  between operations: 14.2 us -> 0.76 us
  starting transfers between devices: 9.32 us -> 3.98 us
  local copies, waits for them, and re-layouts: 1.2 us -> 3.93 us
    pallas_call x0 -> x1, Pallas kernels: none -> 58.9 us  [exchange(): pl.pallas_call(functools.partial(exchange_kernel, experts), out_shape=(ja...]
    all_to_all x1 -> x0, blocking collectives: 57.2 us -> none  [local(): lax.all_to_all(buffer.reshape(experts, per_source, width), 'expert', spli...]
    psum x1 -> x0, waiting for transfers between devices: 15.3 us -> none  [local(): projected_rows = lax.psum(projected_piece, 'tensor')]
    all_to_all x1 -> x0, waiting for transfers between devices: 5 us -> none  [local(): lax.all_to_all(facts, 'expert', split_axis=0, concat_axis=0, tiled=True)]
    all_to_all x1 -> x0, starting transfers between devices: 3.89 us -> none  [local(): lax.all_to_all(facts, 'expert', split_axis=0, concat_axis=0, tiled=True)]
    all_to_all x1, waiting for transfers between devices: 3.16 us -> 0.72 us  [local(): lax.all_to_all(outgoing, ('expert', 'tensor'), split_axis=0, concat_axis=...]
    dot_general x1, matrix products: 3.59 us -> 1.32 us  [local(): lax.dot_general(token_rows, output_map_whole, contract_dims, preferred_el...]
    all_gather x1 -> x0, blocking collectives: 2.18 us -> none  [local(): lax.all_gather(adapter_output_maps[0], 'tensor', axis=1, tiled=True)]
  transfers between devices with their start and end apart: 4 -> 1, of which waited for: 3 -> 1; matrix products, arithmetic and copies ran while one was open for 4% -> 6% of each run, Pallas kernels for 0% -> 0%
where the time goes in v2:
time: 101 us; the launch traced here: 100 us
  Pallas kernels  58.9 us (58%)
  matrix products  28 us (28%)
  starting transfers between devices  3.98 us (4%)
  other arithmetic  3.94 us (4%)
  local copies, waits for them, and re-layouts  3.93 us (4%)
    pallas_call x1, Pallas kernels, exchange(): pl.pallas_call(functools.partial(exchange_kernel, experts), out_shape=(ja...  58.9 us
    dot_general x1, matrix products, local(): lax.dot_general(token_rows, down_matrix[0], contract_dims, preferred_elem...  10.7 us
    all_to_all x1, starting transfers between devices, local(): lax.all_to_all(outgoing, ('expert', 'tensor'), split_axis=0, concat_axis=...  3.98 us
    dot_general x1, matrix products, local(): lax.dot_general(adapter_output.astype(jnp.bfloat16), adapter_input_maps[0...  3.74 us
    dot_general x1, matrix products, local(): jnp.dot(hidden_lowrank, adapter_input_maps[0], preferred_element_type=jnp...  3.64 us
    dot_general x1, matrix products, local(): lax.dot_general(hidden_lowrank, (pick_weight[:, None] * adapter_output).a...  3.39 us
    dot_general x1, matrix products, local(): lax.dot_general((pick_weight[:, None] * projected_rows).astype(jnp.bfloat...  3.03 us
    dot_general x1, matrix products, local(): jnp.dot(filled.astype(jnp.bfloat16), cotangent, preferred_element_type=jn...  2.03 us
  transfers between devices with their start and end apart: 1, of which 1 were waited for; matrix products, arithmetic and copies ran while one was open for 6% of the time, Pallas kernels for 0%

profile of v2, /device:TPU:0, one launch (start us, length us, event | category | flops | bytes accessed | tf_op | source)
XLA Modules:
  0.0 100.3 jit_solution(13911796883032578205)
XLA Ops:
  0.7 0.7 add_convert_fusion
  1.4 0.8 slice_bitcast_fusion.1
  2.1 0.7 convert_reduce_fusion
  2.8 0.1 fusion.47
  3.0 0.7 select_reduce_fusion.5
  3.7 0.7 convert_add_fusion
  4.4 0.3 select_reduce_fusion.3
  4.7 0.1 add.63
  4.7 0.1 reshape.79
  4.8 2.0 %convolution_convert_fusion = bf16[512,2048]{1,0:T(8,128)(2,1)} fusion(bf16[128,2048]{1,0:T(8,128)(2,1)S(1)} %copy-done, s32[128]{0:T(128)S(1)} %get-tuple-element.26, s32[128]{0:T(128)S(1)} %get-tuple-element.25), kind=kOutput, calls=%fused_computation.28 | convolution fusion | flops 269680640 | bytes 2622464 | tf_op jit(solution)/shard_map/dot_general | solution.py:215
  6.9 0.1 pad_maximum_fusion
  6.9 0.6 dynamic_update_slice.3.facts
  7.6 3.6 %fusion.26.piece = f32[512,64]{1,0:T(8,128)} fusion(bf16[1,512,1536]{2,1,0:T(8,128)(2,1)} %param.14, bf16[1,512,1536]{2,1,0:T(8,128)(2,1)} %param.13, bf16[1,1536,64]{1,2,0:T(8,128)(2,1)} %param.16), kind=kOutput, calls=%fused_computation.36 | convolution fusion | flops 106954752 | bytes 3473408 | tf_op jit(solution)/shard_map/dot_general | solution.py:224
  11.2 58.9 %exchange.1 = (bf16[16,32,4096]{2,1,0:T(8,128)(2,1)}, f32[16,8,128]{2,1,0:T(8,128)}, f32[512,64]{1,0:T(8,128)}, bf16[64,4096]{1,0:T(8,128)(2,1)}) custom-call(bf16[16,32,2048]{2,1,0:T(8,128)(2,1)} %bitcast.93, f32[16,8,128]{2,1,0:T(8,128)} %dynamic_update_slice.3.facts, f32[512,64]{1,0:T(8,128)} %fusion.26.piece, bf16[64,2048]{1,0:T(8,128)(2,1)} %bitcast.97), custom_call_target="tpu_custom_call" | custom-call | tf_op jit(solution)/shard_map/exchange/pallas_call | solution.py:143
  70.2 0.8 slice.25
  71.0 0.1 fusion.55
  71.1 0.1 mul.126
  71.2 0.1 eq.69
  71.3 10.7 %fusion = f32[512,1536]{1,0:T(8,128)S(1)} fusion(bf16[512,4096]{1,0:T(8,128)(2,1)} %bitcast.94, bf16[1,1536,4096]{2,1,0:T(8,128)(2,1)} %param.15), kind=kOutput, calls=%fused_computation | convolution fusion | flops 6442450944 | bytes 19922944 | tf_op jit(solution)/shard_map/dot_general | solution.py:251
  82.1 1.3 %fusion.31 = (f32[512]{0:T(512)S(1)}, f32[512,64]{1,0:T(8,128)S(1)}) fusion(f32[512,64]{1,0:T(8,128)S(1)} %copy-done.2, f32[64]{0:T(128)S(1)} %fusion.50, f32[512]{0:T(512)S(1)} %eq.69, bf16[512,4096]{1,0:T(8,128)(2,1)S(1)} %bitcast.96, bf16[64,4096]{1,0:T(8,128)(2,1)S(1)} %copy-done.6), kind=kOutput, calls=%fused_computation.43 | convolution fusion | flops 268598784 | bytes 4985088 | tf_op jit(solution)/shard_map/dot_general | solution.py:258
  83.4 0.0 copy-done.4
  83.4 0.5 copy-done.5
  83.9 3.7 %fusion.25 = (bf16[1,512,1536]{2,1,0:T(8,128)(2,1)}, bf16[1,512,1536]{2,1,0:T(8,128)(2,1)}, f32[512]{0:T(512)S(1)}) fusion(bf16[1,512,1536]{2,1,0:T(8,128)(2,1)S(1)} %copy-done.4, bf16[1,512,1536]{2,1,0:T(8,128)(2,1)S(1)} %copy-done.5, f32[512,1536]{1,0:T(8,128)S(1)} %fusion, bf16[1,1536,64]{1,2,0:T(8,128)(2,1)S(1)} %copy-done.7, ...), kind=kOutput, calls=%fused_computation.35 | convolution fusion | flops 117210624 | bytes 9768960 | tf_op jit(solution)/shard_map/dot_general | solution.py:263
  87.6 0.1 add.69
  87.7 0.6 broadcast_in_dim.81
  88.3 4.0 %all-to-all-start = ((f32[32,1,32]{2,1,0:T(1,128)}), f32[32,1,32]{2,1,0:T(1,128)S(1)}, u32[]{:S(2)}, u32[]{:S(2)}) async-start(f32[32,1,32]{2,1,0:T(1,128)} %bitcast.14), calls=%async_computation | async-start | bytes 32768 | tf_op jit(solution)/shard_map/all_to_all | solution.py:289
  92.3 3.4 %fusion.20 = f32[1,1536,64]{1,2,0:T(8,128)} fusion(bf16[1,512,1536]{2,1,0:T(8,128)(2,1)} %param.14, f32[512,64]{1,0:T(8,128)S(1)} %get-tuple-element.28, f32[512]{0:T(512)S(1)} %mul.126, bf16[1,512,1536]{2,1,0:T(8,128)(2,1)S(1)} %copy-done.4), kind=kOutput, calls=%fused_computation.30 | convolution fusion | flops 107118592 | bytes 3672064 | tf_op jit(solution)/shard_map/dot_general | solution.py:272
  95.7 3.0 %fusion.21 = f32[1,64,2048]{2,1,0:T(8,128)} fusion(bf16[512,4096]{1,0:T(8,128)(2,1)} %bitcast.95, s32[]{:T(128)S(6)} %select_n.35, f32[512,64]{1,0:T(8,128)S(1)} %copy-done.2, f32[512,64]{1,0:T(8,128)S(1)} %copy-done.3, f32[512]{0:T(512)S(1)} %mul.126, f32[64]{0:T(128)S(1)} %fusion.50, f32[512]{0:T(512)S(1)} %eq.69), kind=kOutput, calls=%fused_computation.32 | convolution fusion | flops 134512640 | bytes 2887940 | tf_op jit(solution)/shard_map/dot_general | solution.py:278
  98.7 0.7 all-to-all-done
  99.5 0.1 broadcast_in_dim.82
  99.6 0.2 select_reduce_fusion.1
  99.7 0.6 pad_maximum_fusion.1
  (19 shorter events, 0.1 us)
Async XLA Ops:
  0.6 4.2 %copy-start = (bf16[128,2048]{1,0:T(8,128)(2,1)S(1)}, bf16[128,2048]{1,0:T(8,128)(2,1)}, u32[]{:S(2)}) copy-start(bf16[128,2048]{1,0:T(8,128)(2,1)} %param.9) | copy-start | bytes 1572868
  71.2 10.8 %copy-start.1 = (bf16[16,32,4096]{2,1,0:T(8,128)(2,1)S(1)}, bf16[16,32,4096]{2,1,0:T(8,128)(2,1)}, u32[]{:S(2)}) copy-start(bf16[16,32,4096]{2,1,0:T(8,128)(2,1)} %get-tuple-element.9) | copy-start | bytes 12582916
  71.2 10.8 %copy-start.2 = (f32[512,64]{1,0:T(8,128)S(1)}, f32[512,64]{1,0:T(8,128)}, u32[]{:S(2)}) copy-start(f32[512,64]{1,0:T(8,128)} %fusion.26.piece) | copy-start | bytes 393220
  71.3 10.8 %copy-start.6 = (bf16[64,4096]{1,0:T(8,128)(2,1)S(1)}, bf16[64,4096]{1,0:T(8,128)(2,1)}, u32[]{:S(2)}) copy-start(bf16[64,4096]{1,0:T(8,128)(2,1)} %get-tuple-element.11) | copy-start | bytes 1572868
  82.0 1.4 %copy-start.4 = (bf16[1,512,1536]{2,1,0:T(8,128)(2,1)S(1)}, bf16[1,512,1536]{2,1,0:T(8,128)(2,1)}, u32[]{:S(2)}) copy-start(bf16[1,512,1536]{2,1,0:T(8,128)(2,1)} %param.13) | copy-start | bytes 4718596
  82.0 1.9 %copy-start.5 = (bf16[1,512,1536]{2,1,0:T(8,128)(2,1)S(1)}, bf16[1,512,1536]{2,1,0:T(8,128)(2,1)}, u32[]{:S(2)}) copy-start(bf16[1,512,1536]{2,1,0:T(8,128)(2,1)} %param.14) | copy-start | bytes 4718596
  82.0 1.9 %copy-start.7 = (bf16[1,1536,64]{1,2,0:T(8,128)(2,1)S(1)}, bf16[1,1536,64]{1,2,0:T(8,128)(2,1)}, u32[]{:S(2)}) copy-start(bf16[1,1536,64]{1,2,0:T(8,128)(2,1)} %param.16) | copy-start | bytes 589828
  88.3 11.1 %all-to-all-start = ((f32[32,1,32]{2,1,0:T(1,128)}), f32[32,1,32]{2,1,0:T(1,128)S(1)}, u32[]{:S(2)}, u32[]{:S(2)}) async-start(f32[32,1,32]{2,1,0:T(1,128)} %bitcast.14), calls=%async_computation | async-start | bytes 32768 | tf_op jit(solution)/shard_map/all_to_all | solution.py:289
  92.3 3.4 %copy-start.3 = (f32[512,64]{1,0:T(8,128)S(1)}, f32[512,64]{1,0:T(8,128)}, u32[]{:S(2)}) copy-start(f32[512,64]{1,0:T(8,128)} %get-tuple-element.12) | copy-start | bytes 393220

commit v3 on v2

--- a/solution.py
+++ b/solution.py
@@ -16,16 +16,21 @@
 MESH = pl.DeviceIdType.MESH
 TILE_ROWS = 16
 LANES = 128
+UNIT_TILE = 256
+VMEM_BYTES = 40 * 1024 * 1024
 
 
 def exchange_kernel(
     experts,
     blocks,
     facts,
-    piece,
+    gate,
+    up,
+    input_maps,
     maps,
     rows,
     facts_in,
+    piece,
     other_piece,
     maps_whole,
     row_send,
@@ -107,8 +112,8 @@
         pltpu.make_async_copy(facts.at[expert], facts_in.at[expert], own_sem.at[1]),
         pltpu.make_async_copy(maps, maps_whole.at[:, columns], own_sem.at[2]),
     ]
+    piece_copy = remote(piece, other_piece, pair_send.at[0], pair_recv.at[0], partner)
     pair_copies = [
-        remote(piece, other_piece, pair_send.at[0], pair_recv.at[0], partner),
         remote(maps, maps_whole.at[:, columns], pair_send.at[1], pair_recv.at[1], partner),
         remote(
             blocks.at[expert],
@@ -121,12 +126,24 @@
     for copy in own_copies + pair_copies:
         copy.start()
 
+    part_rows = gate.shape[0] // 4
+
+    @pl.loop(0, 4)
+    def _(index):
+        span = pl.ds(pl.multiple_of(index * part_rows, part_rows), part_rows)
+        hidden = silu_parts(gate[span, :].astype(jnp.float32))[0] * up[span, :].astype(jnp.float32)
+        piece[span, :] = jnp.dot(
+            hidden.astype(jnp.bfloat16), input_maps[...], preferred_element_type=jnp.float32
+        )
+
+    piece_copy.start()
+
     @pl.loop(1, experts)
     def _(step):
         row_copy(step).wait_recv()
         pass_copy(step).start()
 
-    for copy in own_copies + pair_copies:
+    for copy in own_copies + pair_copies + [piece_copy]:
         copy.wait()
 
     @pl.loop(1, experts)
@@ -136,32 +153,143 @@
         pass_copy(step).wait()
 
 
-def exchange(blocks, facts, piece, maps):
+def exchange(blocks, facts, gate, up, input_maps, maps):
     experts, per_source, width = blocks.shape
     anywhere = pl.BlockSpec(memory_space=pl.ANY)
+    vmem = pl.BlockSpec(memory_space=pltpu.VMEM)
     sems = pltpu.SemaphoreType.DMA
     return pl.pallas_call(
         functools.partial(exchange_kernel, experts),
         out_shape=(
             jax.ShapeDtypeStruct((experts, per_source, 2 * width), blocks.dtype),
             jax.ShapeDtypeStruct(facts.shape, facts.dtype),
-            jax.ShapeDtypeStruct(piece.shape, piece.dtype),
+            jax.ShapeDtypeStruct((gate.shape[0], input_maps.shape[1]), jnp.float32),
+            jax.ShapeDtypeStruct((gate.shape[0], input_maps.shape[1]), jnp.float32),
             jax.ShapeDtypeStruct((maps.shape[0], 2 * width), maps.dtype),
         ),
-        in_specs=[anywhere] * 4,
-        out_specs=(anywhere,) * 4,
+        in_specs=[anywhere] * 2 + [vmem] * 3 + [anywhere],
+        out_specs=(anywhere, anywhere, vmem, anywhere, anywhere),
         scratch_shapes=[sems((experts,))] * 6 + [sems((3,))] * 3,
-        compiler_params=pltpu.CompilerParams(collective_id=0, has_side_effects=True),
+        compiler_params=pltpu.CompilerParams(
+            collective_id=0, has_side_effects=True, vmem_limit_bytes=VMEM_BYTES
+        ),
         name="exchange",
-    )(blocks, facts, piece, maps)
-
-
-def fits_exchange(experts, per_source, width):
+    )(blocks, facts, gate, up, input_maps, maps)
+
+
+def gradients_kernel(
+    rows,
+    maps,
+    down,
+    input_maps,
+    gate,
+    up,
+    weight,
+    mask,
+    piece,
+    other_piece,
+    gate_out,
+    up_out,
+    input_out,
+    output_out,
+    slot_out,
+    adapter,
+):
+    contract_dims = (((1,), (1,)), ((), ()))
+    row_dimensions = (((0,), (0,)), ((), ()))
+
+    @pl.when(pl.program_id(0) == 0)
+    def _():
+        adapter[...] = (
+            lax.dot_general(
+                rows[...], maps[...], contract_dims, preferred_element_type=jnp.float32
+            )
+            * mask[...]
+        )
+        projected = (piece[...] + other_piece[...]) * mask[...]
+        width = output_out.shape[1]
+        columns = pl.ds(pl.multiple_of(lax.axis_index("tensor") * width, LANES), width)
+        output_out[...] = adapter_scale * lax.dot_general(
+            (weight[...] * projected).astype(jnp.bfloat16),
+            rows[:, columns],
+            row_dimensions,
+            preferred_element_type=jnp.float32,
+        )
+        slot_out[...] = adapter_scale * jnp.sum(
+            piece[...] * mask[...] * adapter[...], axis=1, keepdims=True
+        )
+
+    base = lax.dot_general(rows[...], down[...], contract_dims, preferred_element_type=jnp.float32)
+    act, slope = silu_parts(gate[...].astype(jnp.float32))
+    up_full = up[...].astype(jnp.float32)
+    hidden = act * up_full
+    slot_out[...] += jnp.sum(hidden * base, axis=1, keepdims=True)
+    backward = lax.dot_general(
+        adapter[...].astype(jnp.bfloat16),
+        input_maps[...],
+        contract_dims,
+        preferred_element_type=jnp.float32,
+    )
+    hidden_gradient = weight[...] * (base + adapter_scale * backward)
+    gate_out[...] = (hidden_gradient * up_full * slope).astype(jnp.bfloat16)
+    up_out[...] = (hidden_gradient * act).astype(jnp.bfloat16)
+    input_out[...] = adapter_scale * lax.dot_general(
+        hidden.astype(jnp.bfloat16),
+        (weight[...] * adapter[...]).astype(jnp.bfloat16),
+        row_dimensions,
+        preferred_element_type=jnp.float32,
+    )
+
+
+def gradients(rows, maps, down, input_maps, gate, up, weight, mask, piece, other_piece):
+    slots, full = rows.shape
+    units = gate.shape[1]
+    columns = maps.shape[0]
+    tile = UNIT_TILE if units % UNIT_TILE == 0 else LANES
+
+    def whole(array):
+        return pl.BlockSpec(array.shape, lambda step: (0, 0))
+
+    by_unit = pl.BlockSpec((slots, tile), lambda step: (0, step))
+    by_row = pl.BlockSpec((tile, columns), lambda step: (step, 0))
+    output_out = jax.ShapeDtypeStruct((columns, full // 2), jnp.float32)
+    slot_out = jax.ShapeDtypeStruct((slots, 1), jnp.float32)
+    return pl.pallas_call(
+        gradients_kernel,
+        grid=(units // tile,),
+        in_specs=[
+            whole(rows),
+            whole(maps),
+            pl.BlockSpec((tile, full), lambda step: (step, 0)),
+            by_row,
+            by_unit,
+            by_unit,
+            whole(weight),
+            whole(mask),
+            whole(piece),
+            whole(other_piece),
+        ],
+        out_specs=(by_unit, by_unit, by_row, whole(output_out), whole(slot_out)),
+        out_shape=(
+            jax.ShapeDtypeStruct(gate.shape, jnp.bfloat16),
+            jax.ShapeDtypeStruct(gate.shape, jnp.bfloat16),
+            jax.ShapeDtypeStruct(input_maps.shape, jnp.float32),
+            output_out,
+            slot_out,
+        ),
+        scratch_shapes=[pltpu.VMEM((slots, columns), jnp.float32)],
+        compiler_params=pltpu.CompilerParams(vmem_limit_bytes=VMEM_BYTES),
+        name="gradients",
+    )(rows, maps, down, input_maps, gate, up, weight, mask, piece, other_piece)
+
+
+def fits_exchange(experts, per_source, width, units):
     return (
         lax.axis_size("tensor") == 2
         and per_source % TILE_ROWS == 0
         and 2 * per_source <= LANES
         and width % LANES == 0
+        and units % LANES == 0
         and experts > 1
     )
 
@@ -215,27 +343,48 @@
     buffer = jnp.dot(
         filled.astype(jnp.bfloat16), cotangent, preferred_element_type=jnp.float32
     ).astype(cotangent.dtype)
-    act, slope = silu_parts(gate_preactivation[0].astype(jnp.float32))
-    up_full = up_preactivation[0].astype(jnp.float32)
-    hidden_units = act * up_full
-    hidden_lowrank = hidden_units.astype(jnp.bfloat16)
-    contract_dims = (((1,), (1,)), ((), ()))
-    row_dimensions = (((0,), (0,)), ((), ()))
-    unmasked_piece = jnp.dot(
-        hidden_lowrank, adapter_input_maps[0], preferred_element_type=jnp.float32
-    )
     blocks = buffer.reshape(experts, per_source, width)
-    if fits_exchange(experts, per_source, width):
+    column_client = jnp.arange(adapter_groups * ADAPTER_RANK, dtype=jnp.int32) // ADAPTER_RANK
+
+    def slot_facts(facts_in):
+        client = facts_in[:, per_source:].reshape(slots, 1)
+        client_mask = (client == (column_client + 1).astype(jnp.float32)).astype(jnp.float32)
+        return facts_in[:, :per_source].reshape(slots, 1), client_mask
+
+    if fits_exchange(experts, per_source, width, gate_preactivation.shape[2]):
         tiles = jnp.zeros((experts, 8, LANES), jnp.float32)
         tiles = lax.dynamic_update_slice(tiles, facts[:, None, :], (0, 0, 0))
-        arrived, tiles_in, other_piece, output_map_whole = exchange(
-            blocks, tiles, unmasked_piece, adapter_output_maps[0]
-        )
-        facts_in = tiles_in[:, 0, : 2 * per_source]
-        token_rows = arrived.reshape(slots, 2 * width)
-        part = lax.dynamic_slice_in_dim(token_rows, lax.axis_index("tensor") * width, width, 1)
-        unmasked_rows = unmasked_piece + other_piece
+        arrived, tiles_in, piece, other_piece, output_map_whole = exchange(
+            blocks,
+            tiles,
+            gate_preactivation[0],
+            up_preactivation[0],
+            adapter_input_maps[0],
+            adapter_output_maps[0],
+        )
+        pick_weight, client_mask = slot_facts(tiles_in[:, 0, : 2 * per_source])
+        gate_gradient, up_gradient, input_map_gradient, output_map_gradient, slot_piece = gradients(
+            arrived.reshape(slots, 2 * width),
+            output_map_whole,
+            down_matrix[0],
+            adapter_input_maps[0],
+            gate_preactivation[0],
+            up_preactivation[0],
+            pick_weight,
+            client_mask,
+            piece,
+            other_piece,
+        )
     else:
+        act, slope = silu_parts(gate_preactivation[0].astype(jnp.float32))
+        up_full = up_preactivation[0].astype(jnp.float32)
+        hidden_units = act * up_full
+        hidden_lowrank = hidden_units.astype(jnp.bfloat16)
+        contract_dims = (((1,), (1,)), ((), ()))
+        row_dimensions = (((0,), (0,)), ((), ()))
+        unmasked_piece = jnp.dot(
+            hidden_lowrank, adapter_input_maps[0], preferred_element_type=jnp.float32
+        )
         facts_in = lax.all_to_all(facts, "expert", split_axis=0, concat_axis=0, tiled=True)
         part = lax.all_to_all(
             blocks, "expert", split_axis=0, concat_axis=0, tiled=True
@@ -243,45 +392,41 @@
         token_rows = lax.all_gather(part, "tensor", axis=1, tiled=True)
         output_map_whole = lax.all_gather(adapter_output_maps[0], "tensor", axis=1, tiled=True)
         unmasked_rows = lax.psum(unmasked_piece, "tensor")
-    pick_weight = facts_in[:, :per_source].reshape(slots)
-    column_client = jnp.arange(adapter_groups * ADAPTER_RANK, dtype=jnp.int32) // ADAPTER_RANK
-    client_mask = (
-        facts_in[:, per_source:].reshape(slots, 1) == (column_client + 1).astype(jnp.float32)
-    ).astype(jnp.float32)
-    frozen_output = lax.dot_general(
-        token_rows, down_matrix[0], contract_dims, preferred_element_type=jnp.float32
-    )
-    projected_piece = unmasked_piece * client_mask
-    projected_rows = unmasked_rows * client_mask
-    local_terms = jnp.sum(hidden_units * frozen_output, axis=1)
-    adapter_output = (
-        lax.dot_general(
-            token_rows, output_map_whole, contract_dims, preferred_element_type=jnp.float32
-        )
-        * client_mask
-    )
-    backward_result = lax.dot_general(
-        adapter_output.astype(jnp.bfloat16),
-        adapter_input_maps[0],
-        contract_dims,
-        preferred_element_type=jnp.float32,
-    )
-    hidden_gradient = pick_weight[:, None] * (frozen_output + adapter_scale * backward_result)
-    gate_gradient = (hidden_gradient * up_full * slope).astype(jnp.bfloat16)
-    up_gradient = (hidden_gradient * act).astype(jnp.bfloat16)
-    input_map_gradient = adapter_scale * lax.dot_general(
-        hidden_lowrank,
-        (pick_weight[:, None] * adapter_output).astype(jnp.bfloat16),
-        row_dimensions,
-        preferred_element_type=jnp.float32,
-    )
-    output_map_gradient = adapter_scale * lax.dot_general(
-        (pick_weight[:, None] * projected_rows).astype(jnp.bfloat16),
-        part,
-        row_dimensions,
-        preferred_element_type=jnp.float32,
-    )
-    slot_piece = local_terms + adapter_scale * jnp.sum(projected_piece * adapter_output, axis=1)
+        pick_weight, client_mask = slot_facts(facts_in)
+        frozen_output = lax.dot_general(
+            token_rows, down_matrix[0], contract_dims, preferred_element_type=jnp.float32
+        )
+        projected_piece = unmasked_piece * client_mask
+        projected_rows = unmasked_rows * client_mask
+        local_terms = jnp.sum(hidden_units * frozen_output, axis=1)
+        adapter_output = (
+            lax.dot_general(
+                token_rows, output_map_whole, contract_dims, preferred_element_type=jnp.float32
+            )
+            * client_mask
+        )
+        backward_result = lax.dot_general(
+            adapter_output.astype(jnp.bfloat16),
+            adapter_input_maps[0],
+            contract_dims,
+            preferred_element_type=jnp.float32,
+        )
+        hidden_gradient = pick_weight * (frozen_output + adapter_scale * backward_result)
+        gate_gradient = (hidden_gradient * up_full * slope).astype(jnp.bfloat16)
+        up_gradient = (hidden_gradient * act).astype(jnp.bfloat16)
+        input_map_gradient = adapter_scale * lax.dot_general(
+            hidden_lowrank,
+            (pick_weight * adapter_output).astype(jnp.bfloat16),
+            row_dimensions,
+            preferred_element_type=jnp.float32,
+        )
+        output_map_gradient = adapter_scale * lax.dot_general(
+            (pick_weight * projected_rows).astype(jnp.bfloat16),
+            part,
+            row_dimensions,
+            preferred_element_type=jnp.float32,
+        )
+        slot_piece = local_terms + adapter_scale * jnp.sum(projected_piece * adapter_output, axis=1)
     tensors = lax.axis_size("tensor")
     outgoing = jnp.broadcast_to(
         slot_piece.reshape(experts, 1, per_source), (experts, tensors, per_source)

time: 101 us -> 107 us (1.059)
  matrix products: 28 us -> 0.84 us
  Pallas kernels: 58.9 us -> 73.1 us
  local copies, waits for them, and re-layouts: 3.93 us -> 16.2 us
  waiting for transfers between devices: 0.72 us -> 6.15 us
  other arithmetic: 3.94 us -> 5.25 us
    dot_general x6 -> x0, matrix products: 25.9 us -> none  [the longest x1 10.7 us: local(): lax.dot_general(token_rows, down_matrix[0], contract_dims, preferred_elem...]
    pallas_call x0 -> x1, Pallas kernels: none -> 14.5 us  [gradients(): pl.pallas_call(gradients_kernel, grid=(units // tile,), in_specs=[whole(r...]
    unnamed x16 -> x30, local copies, waits for them, and re-layouts: 0.54 us -> 14.1 us
    all_to_all x1, waiting for transfers between devices: 0.72 us -> 6.15 us  [local(): lax.all_to_all(outgoing, ('expert', 'tensor'), split_axis=0, concat_axis=...]
    dot_general x1, matrix products: 2.03 us -> 0.7 us  [local(): jnp.dot(filled.astype(jnp.bfloat16), cotangent, preferred_element_type=jn...]
    pallas_call x0 -> x1, other arithmetic: none -> 1.09 us  [gradients(): pl.pallas_call(gradients_kernel, grid=(units // tile,), in_specs=[whole(r...]
  transfers between devices with their start and end apart: 1 -> 1, of which waited for: 1 -> 1; matrix products, arithmetic and copies ran while one was open for 6% -> 1% of each run, Pallas kernels for 0% -> 0%
where the time goes in v3:
time: 107 us; the launch traced here: 106 us
  Pallas kernels  73.1 us (68%)
  local copies, waits for them, and re-layouts  16.2 us (15%)
  waiting for transfers between devices  6.15 us (6%)
  other arithmetic  5.25 us (5%)
  starting transfers between devices  3.64 us (3%)
    pallas_call x1, Pallas kernels, exchange(): pl.pallas_call(functools.partial(exchange_kernel, experts), out_shape=(ja...  58.6 us
    pallas_call x1, Pallas kernels, gradients(): pl.pallas_call(gradients_kernel, grid=(units // tile,), in_specs=[whole(r...  14.5 us
    unnamed x30, local copies, waits for them, and re-layouts  14.1 us
    all_to_all x1, waiting for transfers between devices, local(): lax.all_to_all(outgoing, ('expert', 'tensor'), split_axis=0, concat_axis=...  6.15 us
    all_to_all x1, starting transfers between devices, local(): lax.all_to_all(outgoing, ('expert', 'tensor'), split_axis=0, concat_axis=...  3.64 us
  transfers between devices with their start and end apart: 1, of which 1 were waited for; matrix products, arithmetic and copies ran while one was open for 1% of the time, Pallas kernels for 0%

profile of v3, /device:TPU:0, one launch (start us, length us, event | category | flops | bytes accessed | tf_op | source)
XLA Modules:
  0.0 106.0 jit_solution(16242187211495552665)
XLA Ops:
  0.7 0.8 add_convert_fusion
  1.5 0.8 slice_bitcast_fusion.1
  2.2 0.7 convert_reduce_fusion
  2.9 0.1 fusion.4
  3.1 0.7 select_reduce_fusion.5
  3.8 0.7 convert_add_fusion
  4.5 0.3 select_reduce_fusion.3
  4.9 1.1 %copy.28 = bf16[1,1536,64]{2,1,0:T(8,128)(2,1)S(1)} copy(bf16[1,1536,64]{1,2,0:T(8,128)(2,1)} %param.16) | data formatting | bytes 393216 | tf_op args[7]
  6.1 0.7 convolution_convert_fusion
  6.9 0.6 copy-done.2
  7.5 58.6 %exchange.1 = (bf16[16,32,4096]{2,1,0:T(8,128)(2,1)S(1)}, f32[16,8,128]{2,1,0:T(8,128)S(1)}, f32[512,64]{1,0:T(8,128)S(1)}, f32[512,64]{1,0:T(8,128)S(1)}, bf16[64,4096]{1,0:T(8,128)(2,1)S(1)}) custom-call(bf16[16,32,2048]{2,1,0:T(8,128)(2,1)S(1)} %bitcast.27, f32[16,8,128]{2,1,0:T(8,128)S(1)} %dynamic_update_slice.3.facts, bf16[512,1536]{1,0:T(8,128)(2,1)S(1)} %bitcast.28, ...), custom_call_target="tpu_custom_call" | custom-call | tf_op jit(solution)/shard_map/exchange/pallas_call | solution.py:161
  66.2 1.9 %copy-done.4 = bf16[16,32,4096]{2,1,0:T(8,128)(2,1)} copy-done((bf16[16,32,4096]{2,1,0:T(8,128)(2,1)}, bf16[16,32,4096]{2,1,0:T(8,128)(2,1)S(1)}, u32[]{:S(2)}) %copy-start.4) | copy-done | bytes 4194328
  68.1 0.8 copy-done.6
  68.9 0.7 copy-done.8
  69.6 0.7 copy-done.10
  70.4 0.1 eq.69
  70.4 0.3 reshape.68.weight
  70.7 0.1 compare_convert_fusion.mask
  70.9 1.4 %copy-done.3 = bf16[1,512,1536]{2,1,0:T(8,128)(2,1)S(1)} copy-done((bf16[1,512,1536]{2,1,0:T(8,128)(2,1)S(1)}, bf16[1,512,1536]{2,1,0:T(8,128)(2,1)}, u32[]{:S(2)}) %copy-start.3) | copy-done | bytes 1572888
  72.3 2.2 %copy-done.5 = bf16[16,32,4096]{2,1,0:T(8,128)(2,1)S(1)} copy-done((bf16[16,32,4096]{2,1,0:T(8,128)(2,1)S(1)}, bf16[16,32,4096]{2,1,0:T(8,128)(2,1)}, u32[]{:S(2)}) %copy-start.5) | copy-done | bytes 4194328
  74.4 1.0 copy-done.7
  75.5 0.9 copy-done.9
  76.4 0.9 copy-done.11
  77.4 14.5 %gradients.1 = (bf16[512,1536]{1,0:T(8,128)(2,1)}, bf16[512,1536]{1,0:T(8,128)(2,1)}, f32[1536,64]{1,0:T(8,128)S(1)}, f32[64,2048]{1,0:T(8,128)}, f32[512,1]{1,0:T(8,128)S(1)}) custom-call(bf16[512,4096]{1,0:T(8,128)(2,1)S(1)} %bitcast.32, bf16[64,4096]{1,0:T(8,128)(2,1)S(1)} %copy-done.7, bf16[1536,4096]{1,0:T(8,128)(2,1)} %bitcast.37, ...), custom_call_target="tpu_custom_call" | custom-call | tf_op jit(solution)/shard_map/gradients/pallas_call | solution.py:257
  91.9 0.7 copy-done.13
  92.6 1.1 %reduce = f32[512]{0:T(512)S(1)} reduce(f32[512,1]{1,0:T(8,128)} %copy-done.13, f32[]{:T(128)} %constant.34), dimensions={1}, to_apply=%get-tuple-element.20.reduce_sub_computation | reduce | bytes 4100 | tf_op jit(solution)/shard_map/gradients/pallas_call | solution.py:257
  93.8 0.6 broadcast_in_dim.84
  94.4 3.6 %all-to-all-start = ((f32[32,1,32]{2,1,0:T(1,128)}), f32[32,1,32]{2,1,0:T(1,128)S(1)}, u32[]{:S(2)}, u32[]{:S(2)}) async-start(f32[32,1,32]{2,1,0:T(1,128)} %bitcast.13), calls=%async_computation | async-start | bytes 32768 | tf_op jit(solution)/shard_map/all_to_all | solution.py:434
  98.0 1.0 copy.30
  99.0 6.1 %all-to-all-done = f32[32,1,32]{2,1,0:T(1,128)S(1)} async-done(((f32[32,1,32]{2,1,0:T(1,128)}), f32[32,1,32]{2,1,0:T(1,128)S(1)}, u32[]{:S(2)}, u32[]{:S(2)}) %all-to-all-start) | async-done | bytes 4128 | tf_op jit(solution)/shard_map/all_to_all | solution.py:434
  105.3 0.2 select_reduce_fusion.1
  105.5 0.6 pad_maximum_fusion.1
  (29 shorter events, 0.6 us)
Async XLA Ops:
  0.6 5.5 %copy-start = (bf16[128,2048]{1,0:T(8,128)(2,1)S(1)}, bf16[128,2048]{1,0:T(8,128)(2,1)}, u32[]{:S(2)}) copy-start(bf16[128,2048]{1,0:T(8,128)(2,1)} %param.9) | copy-start | bytes 1572868
  0.6 6.3 %copy-start.12 = (bf16[1,64,2048]{2,1,0:T(8,128)(2,1)S(1)}, bf16[1,64,2048]{2,1,0:T(8,128)(2,1)}, u32[]{:S(2)}) copy-start(bf16[1,64,2048]{2,1,0:T(8,128)(2,1)} %param.17) | copy-start | bytes 786436
  0.7 6.3 %copy-start.1 = (bf16[1,512,1536]{2,1,0:T(8,128)(2,1)S(1)}, bf16[1,512,1536]{2,1,0:T(8,128)(2,1)}, u32[]{:S(2)}) copy-start(bf16[1,512,1536]{2,1,0:T(8,128)(2,1)} %param.13) | copy-start | bytes 4718596
  6.1 1.4 %copy-start.2 = (bf16[1,512,1536]{2,1,0:T(8,128)(2,1)S(1)}, bf16[1,512,1536]{2,1,0:T(8,128)(2,1)}, u32[]{:S(2)}) copy-start(bf16[1,512,1536]{2,1,0:T(8,128)(2,1)} %param.14) | copy-start | bytes 4718596
  66.1 1.9 %copy-start.4 = (bf16[16,32,4096]{2,1,0:T(8,128)(2,1)}, bf16[16,32,4096]{2,1,0:T(8,128)(2,1)S(1)}, u32[]{:S(2)}) copy-start(bf16[16,32,4096]{2,1,0:T(8,128)(2,1)S(1)} %get-tuple-element.15) | copy-start | bytes 12582916
  68.1 0.8 copy-start.6
  68.9 0.7 copy-start.8
  69.6 0.7 copy-start.10
  70.8 1.4 %copy-start.3 = (bf16[1,512,1536]{2,1,0:T(8,128)(2,1)S(1)}, bf16[1,512,1536]{2,1,0:T(8,128)(2,1)}, u32[]{:S(2)}) copy-start(bf16[1,512,1536]{2,1,0:T(8,128)(2,1)} %param.14) | copy-start | bytes 4718596
  72.2 2.2 %copy-start.5 = (bf16[16,32,4096]{2,1,0:T(8,128)(2,1)S(1)}, bf16[16,32,4096]{2,1,0:T(8,128)(2,1)}, u32[]{:S(2)}) copy-start(bf16[16,32,4096]{2,1,0:T(8,128)(2,1)} %copy-done.4) | copy-start | bytes 12582916
  74.4 1.0 copy-start.7
  75.5 0.9 copy-start.9
  76.4 0.9 copy-start.11
  91.9 0.7 copy-start.13
  94.4 10.8 %all-to-all-start = ((f32[32,1,32]{2,1,0:T(1,128)}), f32[32,1,32]{2,1,0:T(1,128)S(1)}, u32[]{:S(2)}, u32[]{:S(2)}) async-start(f32[32,1,32]{2,1,0:T(1,128)} %bitcast.13), calls=%async_computation | async-start | bytes 32768 | tf_op jit(solution)/shard_map/all_to_all | solution.py:434

commit v4 on v3

--- a/solution.py
+++ b/solution.py
@@ -17,7 +17,7 @@
 TILE_ROWS = 16
 LANES = 128
 UNIT_TILE = 256
-VMEM_BYTES = 40 * 1024 * 1024
+VMEM_BYTES = 60 * 1024 * 1024
 
 
 def exchange_kernel(

time: 107 us -> 105 us (0.981)
  local copies, waits for them, and re-layouts: 16.2 us -> 8.3 us
  Pallas kernels: 73.1 us -> 78.4 us
  matrix products: 0.84 us -> 2.17 us
  waiting for transfers between devices: 6.15 us -> 5.01 us
    unnamed x30 -> x4, local copies, waits for them, and re-layouts: 14.1 us -> 3.99 us
    pallas_call x1, Pallas kernels: 58.6 us -> 61.6 us  [exchange(): pl.pallas_call(functools.partial(exchange_kernel, experts), out_shape=(ja...]
    pallas_call x1, Pallas kernels: 14.5 us -> 16.8 us  [gradients(): pl.pallas_call(gradients_kernel, grid=(units // tile,), in_specs=[whole(r...]
    dot_general x1, matrix products: 0.7 us -> 2.03 us  [local(): jnp.dot(filled.astype(jnp.bfloat16), cotangent, preferred_element_type=jn...]
    all_to_all x1, waiting for transfers between devices: 6.15 us -> 5.01 us  [local(): lax.all_to_all(outgoing, ('expert', 'tensor'), split_axis=0, concat_axis=...]
  transfers between devices with their start and end apart: 1 -> 1, of which waited for: 1 -> 1; matrix products, arithmetic and copies ran while one was open for 1% -> 2% of each run, Pallas kernels for 0% -> 0%
where the time goes in v4:
time: 105 us; the launch traced here: 104 us
  Pallas kernels  78.4 us (75%)
  local copies, waits for them, and re-layouts  8.3 us (8%)
  other arithmetic  5.87 us (6%)
  waiting for transfers between devices  5.01 us (5%)
  starting transfers between devices  3.95 us (4%)
  matrix products  2.17 us (2%)
    pallas_call x1, Pallas kernels, exchange(): pl.pallas_call(functools.partial(exchange_kernel, experts), out_shape=(ja...  61.6 us
    pallas_call x1, Pallas kernels, gradients(): pl.pallas_call(gradients_kernel, grid=(units // tile,), in_specs=[whole(r...  16.8 us
    all_to_all x1, waiting for transfers between devices, local(): lax.all_to_all(outgoing, ('expert', 'tensor'), split_axis=0, concat_axis=...  5.01 us
    unnamed x4, local copies, waits for them, and re-layouts  3.99 us
    all_to_all x1, starting transfers between devices, local(): lax.all_to_all(outgoing, ('expert', 'tensor'), split_axis=0, concat_axis=...  3.95 us
  transfers between devices with their start and end apart: 1, of which 1 were waited for; matrix products, arithmetic and copies ran while one was open for 2% of the time, Pallas kernels for 0%

profile of v4, /device:TPU:0, one launch (start us, length us, event | category | flops | bytes accessed | tf_op | source)
XLA Modules:
  0.0 104.4 jit_solution(14401393750876272744)
XLA Ops:
  0.6 0.0 copy-start
  0.7 0.7 add_convert_fusion
  1.4 0.8 slice_bitcast_fusion.1
  2.1 0.7 convert_reduce_fusion
  2.8 0.1 fusion.4
  3.0 0.7 select_reduce_fusion.5
  3.7 0.7 convert_add_fusion
  4.4 0.3 select_reduce_fusion.3
  4.7 0.1 add.34
  4.7 0.1 reshape.64
  4.8 1.9 %copy.28 = bf16[1,1536,64]{2,1,0:T(8,128)(2,1)} copy(bf16[1,1536,64]{1,2,0:T(8,128)(2,1)} %param.16) | data formatting | bytes 393216 | tf_op args[7]
  6.7 0.0 copy-done
  6.7 2.0 %convolution_convert_fusion = bf16[512,2048]{1,0:T(8,128)(2,1)} fusion(bf16[128,2048]{1,0:T(8,128)(2,1)S(1)} %copy-done, s32[128]{0:T(128)S(1)} %get-tuple-element.55, s32[128]{0:T(128)S(1)} %get-tuple-element.54), kind=kOutput, calls=%fused_computation | convolution fusion | flops 269680640 | bytes 2622464 | tf_op jit(solution)/shard_map/dot_general | solution.py:343
  8.7 0.1 pad_maximum_fusion
  8.8 0.6 dynamic_update_slice.3.facts
  9.4 61.6 %exchange.1 = (bf16[16,32,4096]{2,1,0:T(8,128)(2,1)}, f32[16,8,128]{2,1,0:T(8,128)}, f32[512,64]{1,0:T(8,128)}, f32[512,64]{1,0:T(8,128)}, bf16[64,4096]{1,0:T(8,128)(2,1)}) custom-call(bf16[16,32,2048]{2,1,0:T(8,128)(2,1)} %bitcast.28, f32[16,8,128]{2,1,0:T(8,128)} %dynamic_update_slice.3.facts, bf16[512,1536]{1,0:T(8,128)(2,1)} %bitcast.29, ...), custom_call_target="tpu_custom_call" | custom-call | tf_op jit(solution)/shard_map/exchange/pallas_call | solution.py:161
  71.0 0.8 slice.25
  71.9 0.1 fusion.8
  72.0 0.1 eq.69
  72.0 1.0 reshape.68.weight
  73.0 0.8 compare_convert_fusion.mask
  73.9 16.8 %gradients.1 = (bf16[512,1536]{1,0:T(8,128)(2,1)}, bf16[512,1536]{1,0:T(8,128)(2,1)}, f32[1536,64]{1,0:T(8,128)}, f32[64,2048]{1,0:T(8,128)}, f32[512,1]{1,0:T(8,128)}) custom-call(bf16[512,4096]{1,0:T(8,128)(2,1)} %bitcast.33, bf16[64,4096]{1,0:T(8,128)(2,1)} %get-tuple-element.16.maps, bf16[1536,4096]{1,0:T(8,128)(2,1)} %bitcast.27, ...), custom_call_target="tpu_custom_call" | custom-call | tf_op jit(solution)/shard_map/gradients/pallas_call | solution.py:257
  90.7 1.1 %reduce = f32[512]{0:T(512)S(1)} reduce(f32[512,1]{1,0:T(8,128)} %get-tuple-element.20, f32[]{:T(128)} %constant.34), dimensions={1}, to_apply=%get-tuple-element.20.reduce_sub_computation | reduce | bytes 4100 | tf_op jit(solution)/shard_map/gradients/pallas_call | solution.py:257
  91.8 0.1 broadcast_in_dim.83
  91.8 0.6 broadcast_in_dim.84
  92.5 4.0 %all-to-all-start = ((f32[32,1,32]{2,1,0:T(1,128)}), f32[32,1,32]{2,1,0:T(1,128)S(1)}, u32[]{:S(2)}, u32[]{:S(2)}) async-start(f32[32,1,32]{2,1,0:T(1,128)} %bitcast.13), calls=%async_computation | async-start | bytes 32768 | tf_op jit(solution)/shard_map/all_to_all | solution.py:434
  96.4 2.1 %copy.30 = f32[1,1536,64]{1,2,0:T(8,128)} copy(f32[1,1536,64]{2,1,0:T(8,128)} %bitcast.36) | data formatting | bytes 786432
  98.5 5.0 %all-to-all-done = f32[32,1,32]{2,1,0:T(1,128)S(1)} async-done(((f32[32,1,32]{2,1,0:T(1,128)}), f32[32,1,32]{2,1,0:T(1,128)S(1)}, u32[]{:S(2)}, u32[]{:S(2)}) %all-to-all-start) | async-done | bytes 4128 | tf_op jit(solution)/shard_map/all_to_all | solution.py:434
  103.6 0.1 broadcast_in_dim.85
  103.7 0.2 select_reduce_fusion.1
  103.8 0.6 pad_maximum_fusion.1
  (4 shorter events, 0.0 us)
Async XLA Ops:
  0.6 6.0 %copy-start = (bf16[128,2048]{1,0:T(8,128)(2,1)S(1)}, bf16[128,2048]{1,0:T(8,128)(2,1)}, u32[]{:S(2)}) copy-start(bf16[128,2048]{1,0:T(8,128)(2,1)} %param.9) | copy-start | bytes 1572868
  92.5 11.1 %all-to-all-start = ((f32[32,1,32]{2,1,0:T(1,128)}), f32[32,1,32]{2,1,0:T(1,128)S(1)}, u32[]{:S(2)}, u32[]{:S(2)}) async-start(f32[32,1,32]{2,1,0:T(1,128)} %bitcast.13), calls=%async_computation | async-start | bytes 32768 | tf_op jit(solution)/shard_map/all_to_all | solution.py:434

commit v5 on v2

--- a/solution.py
+++ b/solution.py
@@ -94,9 +94,12 @@
             partner,
         )
 
-    @pl.loop(1, experts)
-    def _(step):
-        row_copy(step).start()
+    def far_first(index):
+        return experts // 2 + (1 - 2 * (index % 2)) * ((index + 1) // 2)
+
+    @pl.loop(0, experts - 1)
+    def _(index):
+        row_copy(far_first(index)).start()
 
     @pl.loop(1, experts)
     def _(step):
@@ -121,10 +124,10 @@
     for copy in own_copies + pair_copies:
         copy.start()
 
-    @pl.loop(1, experts)
-    def _(step):
-        row_copy(step).wait_recv()
-        pass_copy(step).start()
+    @pl.loop(0, experts - 1)
+    def _(index):
+        row_copy(far_first(index)).wait_recv()
+        pass_copy(far_first(index)).start()
 
     for copy in own_copies + pair_copies:
         copy.wait()
@@ -162,7 +165,7 @@
         and per_source % TILE_ROWS == 0
         and 2 * per_source <= LANES
         and width % LANES == 0
-        and experts > 1
+        and experts % 2 == 0
     )
 
 

time: 101 us -> 99.5 us (0.985)
    pallas_call x1, Pallas kernels: 58.9 us -> 57.9 us  [exchange(): pl.pallas_call(functools.partial(exchange_kernel, experts), out_shape=(ja...]
where the time goes in v5:
time: 99.5 us; the launch traced here: 99.2 us
  Pallas kernels  57.9 us (58%)
  matrix products  28 us (28%)
  other arithmetic  3.94 us (4%)
  local copies, waits for them, and re-layouts  3.93 us (4%)
  starting transfers between devices  3.89 us (4%)
    pallas_call x1, Pallas kernels, exchange(): pl.pallas_call(functools.partial(exchange_kernel, experts), out_shape=(ja...  57.9 us
    dot_general x1, matrix products, local(): lax.dot_general(token_rows, down_matrix[0], contract_dims, preferred_elem...  10.7 us
    all_to_all x1, starting transfers between devices, local(): lax.all_to_all(outgoing, ('expert', 'tensor'), split_axis=0, concat_axis=...  3.89 us
    dot_general x1, matrix products, local(): lax.dot_general(adapter_output.astype(jnp.bfloat16), adapter_input_maps[0...  3.75 us
    dot_general x1, matrix products, local(): jnp.dot(hidden_lowrank, adapter_input_maps[0], preferred_element_type=jnp...  3.64 us
    dot_general x1, matrix products, local(): lax.dot_general(hidden_lowrank, (pick_weight[:, None] * adapter_output).a...  3.38 us
    dot_general x1, matrix products, local(): lax.dot_general((pick_weight[:, None] * projected_rows).astype(jnp.bfloat...  3.03 us
    dot_general x1, matrix products, local(): jnp.dot(filled.astype(jnp.bfloat16), cotangent, preferred_element_type=jn...  2.03 us
  transfers between devices with their start and end apart: 1, of which 1 were waited for; matrix products, arithmetic and copies ran while one was open for 6% of the time, Pallas kernels for 0%

profile of v5, /device:TPU:0, one launch (start us, length us, event | category | flops | bytes accessed | tf_op | source)
XLA Modules:
  0.0 99.2 jit_solution(9516617695169445721)
XLA Ops:
  0.7 0.7 add_convert_fusion
  1.4 0.8 slice_bitcast_fusion.1
  2.1 0.7 convert_reduce_fusion
  2.8 0.1 fusion.47
  3.0 0.7 select_reduce_fusion.5
  3.7 0.7 convert_add_fusion
  4.4 0.3 select_reduce_fusion.3
  4.7 0.1 add.63
  4.7 0.1 reshape.79
  4.8 2.0 %convolution_convert_fusion = bf16[512,2048]{1,0:T(8,128)(2,1)} fusion(bf16[128,2048]{1,0:T(8,128)(2,1)S(1)} %copy-done, s32[128]{0:T(128)S(1)} %get-tuple-element.26, s32[128]{0:T(128)S(1)} %get-tuple-element.25), kind=kOutput, calls=%fused_computation.28 | convolution fusion | flops 269680640 | bytes 2622464 | tf_op jit(solution)/shard_map/dot_general | solution.py:218
  6.9 0.1 pad_maximum_fusion
  6.9 0.6 dynamic_update_slice.3.facts
  7.6 3.6 %fusion.26.piece = f32[512,64]{1,0:T(8,128)} fusion(bf16[1,512,1536]{2,1,0:T(8,128)(2,1)} %param.14, bf16[1,512,1536]{2,1,0:T(8,128)(2,1)} %param.13, bf16[1,1536,64]{1,2,0:T(8,128)(2,1)} %param.16), kind=kOutput, calls=%fused_computation.36 | convolution fusion | flops 106954752 | bytes 3473408 | tf_op jit(solution)/shard_map/dot_general | solution.py:227
  11.2 57.9 %exchange.1 = (bf16[16,32,4096]{2,1,0:T(8,128)(2,1)}, f32[16,8,128]{2,1,0:T(8,128)}, f32[512,64]{1,0:T(8,128)}, bf16[64,4096]{1,0:T(8,128)(2,1)}) custom-call(bf16[16,32,2048]{2,1,0:T(8,128)(2,1)} %bitcast.93, f32[16,8,128]{2,1,0:T(8,128)} %dynamic_update_slice.3.facts, f32[512,64]{1,0:T(8,128)} %fusion.26.piece, bf16[64,2048]{1,0:T(8,128)(2,1)} %bitcast.97), custom_call_target="tpu_custom_call" | custom-call | tf_op jit(solution)/shard_map/exchange/pallas_call | solution.py:146
  69.1 0.8 slice.25
  70.0 0.1 fusion.55
  70.0 0.1 mul.126
  70.1 0.1 eq.69
  70.2 10.7 %fusion = f32[512,1536]{1,0:T(8,128)S(1)} fusion(bf16[512,4096]{1,0:T(8,128)(2,1)} %bitcast.94, bf16[1,1536,4096]{2,1,0:T(8,128)(2,1)} %param.15), kind=kOutput, calls=%fused_computation | convolution fusion | flops 6442450944 | bytes 19922944 | tf_op jit(solution)/shard_map/dot_general | solution.py:254
  81.0 1.3 %fusion.31 = (f32[512]{0:T(512)S(1)}, f32[512,64]{1,0:T(8,128)S(1)}) fusion(f32[512,64]{1,0:T(8,128)S(1)} %copy-done.2, f32[64]{0:T(128)S(1)} %fusion.50, f32[512]{0:T(512)S(1)} %eq.69, bf16[512,4096]{1,0:T(8,128)(2,1)S(1)} %bitcast.96, bf16[64,4096]{1,0:T(8,128)(2,1)S(1)} %copy-done.6), kind=kOutput, calls=%fused_computation.43 | convolution fusion | flops 268598784 | bytes 4985088 | tf_op jit(solution)/shard_map/dot_general | solution.py:261
  82.3 0.0 copy-done.4
  82.4 0.5 copy-done.5
  82.8 3.8 %fusion.25 = (bf16[1,512,1536]{2,1,0:T(8,128)(2,1)}, bf16[1,512,1536]{2,1,0:T(8,128)(2,1)}, f32[512]{0:T(512)S(1)}) fusion(bf16[1,512,1536]{2,1,0:T(8,128)(2,1)S(1)} %copy-done.4, bf16[1,512,1536]{2,1,0:T(8,128)(2,1)S(1)} %copy-done.5, f32[512,1536]{1,0:T(8,128)S(1)} %fusion, bf16[1,1536,64]{1,2,0:T(8,128)(2,1)S(1)} %copy-done.7, ...), kind=kOutput, calls=%fused_computation.35 | convolution fusion | flops 117210624 | bytes 9768960 | tf_op jit(solution)/shard_map/dot_general | solution.py:266
  86.6 0.1 add.69
  86.7 0.6 broadcast_in_dim.81
  87.3 3.9 %all-to-all-start = ((f32[32,1,32]{2,1,0:T(1,128)}), f32[32,1,32]{2,1,0:T(1,128)S(1)}, u32[]{:S(2)}, u32[]{:S(2)}) async-start(f32[32,1,32]{2,1,0:T(1,128)} %bitcast.14), calls=%async_computation | async-start | bytes 32768 | tf_op jit(solution)/shard_map/all_to_all | solution.py:292
  91.2 3.4 %fusion.20 = f32[1,1536,64]{1,2,0:T(8,128)} fusion(bf16[1,512,1536]{2,1,0:T(8,128)(2,1)} %param.14, f32[512,64]{1,0:T(8,128)S(1)} %get-tuple-element.28, f32[512]{0:T(512)S(1)} %mul.126, bf16[1,512,1536]{2,1,0:T(8,128)(2,1)S(1)} %copy-done.4), kind=kOutput, calls=%fused_computation.30 | convolution fusion | flops 107118592 | bytes 3672064 | tf_op jit(solution)/shard_map/dot_general | solution.py:275
  94.6 3.0 %fusion.21 = f32[1,64,2048]{2,1,0:T(8,128)} fusion(bf16[512,4096]{1,0:T(8,128)(2,1)} %bitcast.95, s32[]{:T(128)S(6)} %select_n.35, f32[512,64]{1,0:T(8,128)S(1)} %copy-done.2, f32[512,64]{1,0:T(8,128)S(1)} %copy-done.3, f32[512]{0:T(512)S(1)} %mul.126, f32[64]{0:T(128)S(1)} %fusion.50, f32[512]{0:T(512)S(1)} %eq.69), kind=kOutput, calls=%fused_computation.32 | convolution fusion | flops 134512640 | bytes 2887940 | tf_op jit(solution)/shard_map/dot_general | solution.py:281
  97.6 0.7 all-to-all-done
  98.4 0.1 broadcast_in_dim.82
  98.4 0.2 select_reduce_fusion.1
  98.6 0.6 pad_maximum_fusion.1
  (19 shorter events, 0.1 us)
Async XLA Ops:
  0.6 4.2 %copy-start = (bf16[128,2048]{1,0:T(8,128)(2,1)S(1)}, bf16[128,2048]{1,0:T(8,128)(2,1)}, u32[]{:S(2)}) copy-start(bf16[128,2048]{1,0:T(8,128)(2,1)} %param.9) | copy-start | bytes 1572868
  70.2 10.8 %copy-start.1 = (bf16[16,32,4096]{2,1,0:T(8,128)(2,1)S(1)}, bf16[16,32,4096]{2,1,0:T(8,128)(2,1)}, u32[]{:S(2)}) copy-start(bf16[16,32,4096]{2,1,0:T(8,128)(2,1)} %get-tuple-element.9) | copy-start | bytes 12582916
  70.2 10.8 %copy-start.2 = (f32[512,64]{1,0:T(8,128)S(1)}, f32[512,64]{1,0:T(8,128)}, u32[]{:S(2)}) copy-start(f32[512,64]{1,0:T(8,128)} %fusion.26.piece) | copy-start | bytes 393220
  70.2 10.8 %copy-start.6 = (bf16[64,4096]{1,0:T(8,128)(2,1)S(1)}, bf16[64,4096]{1,0:T(8,128)(2,1)}, u32[]{:S(2)}) copy-start(bf16[64,4096]{1,0:T(8,128)(2,1)} %get-tuple-element.11) | copy-start | bytes 1572868
  80.9 1.4 %copy-start.4 = (bf16[1,512,1536]{2,1,0:T(8,128)(2,1)S(1)}, bf16[1,512,1536]{2,1,0:T(8,128)(2,1)}, u32[]{:S(2)}) copy-start(bf16[1,512,1536]{2,1,0:T(8,128)(2,1)} %param.13) | copy-start | bytes 4718596
  81.0 1.9 %copy-start.5 = (bf16[1,512,1536]{2,1,0:T(8,128)(2,1)S(1)}, bf16[1,512,1536]{2,1,0:T(8,128)(2,1)}, u32[]{:S(2)}) copy-start(bf16[1,512,1536]{2,1,0:T(8,128)(2,1)} %param.14) | copy-start | bytes 4718596
  81.0 1.9 %copy-start.7 = (bf16[1,1536,64]{1,2,0:T(8,128)(2,1)S(1)}, bf16[1,1536,64]{1,2,0:T(8,128)(2,1)}, u32[]{:S(2)}) copy-start(bf16[1,1536,64]{1,2,0:T(8,128)(2,1)} %param.16) | copy-start | bytes 589828
  87.3 11.0 %all-to-all-start = ((f32[32,1,32]{2,1,0:T(1,128)}), f32[32,1,32]{2,1,0:T(1,128)S(1)}, u32[]{:S(2)}, u32[]{:S(2)}) async-start(f32[32,1,32]{2,1,0:T(1,128)} %bitcast.14), calls=%async_computation | async-start | bytes 32768 | tf_op jit(solution)/shard_map/all_to_all | solution.py:292
  91.2 3.4 %copy-start.3 = (f32[512,64]{1,0:T(8,128)S(1)}, f32[512,64]{1,0:T(8,128)}, u32[]{:S(2)}) copy-start(f32[512,64]{1,0:T(8,128)} %get-tuple-element.12) | copy-start | bytes 393220
